TPU v7x, 32 devices: a whole 2x2x4 slice. The times are simulated.
32 devices in a mesh: groups: 2 (over x), seq: 16 (over z, y, core).
Axes of the slice: x: 2, y: 2, z: 4, core: 2. Of those that a mesh axis runs over, the one named last changes fastest.
Arguments:
- queries: bfloat16 [24576, 2560], P(('groups', 'seq')), parts along dimension 0, may hold values from -30 to 30
- keys: bfloat16 [24576, 2560], P(('groups', 'seq')), parts along dimension 0, may hold values from -30 to 30
- values: bfloat16 [24576, 2560], P(('groups', 'seq')), parts along dimension 0, may hold values from -18 to 18
- lengths: int32 [16], P('groups'), parts along dimension 0, may hold values from 1 to 1536, as said below
- help_table: int32 [32, 2], P(('groups', 'seq')), parts along dimension 0, may hold values from -1 to 5, as said below
Outputs:
- attended: bfloat16 [24576, 2560], P(('groups', 'seq')), parts along dimension 0
- helped: bfloat16 [8192, 2560], P(('groups', 'seq')), parts along dimension 0
There are 2 independent parts, one for each index of `groups`. A program takes and returns all parts, laid end to end along the dimension named above; each array names one. Nothing has to cross between parts.
Inputs may be any that keep to these rules, and one draw needn't show every extreme that they name: `lengths`: in each pair of candidates m, m + 4 one has more than 1408 valid tokens and the other at most 768; some candidate has exactly 1536 and some exactly 768. `help_table`: a device whose candidate is the shorter of its pair lists 2 distinct slab indices of its pair device; every other device has -1 in all slots.
All inputs are finite; a program needn't handle non-finite values.
Results may differ from a plain program's by a relative error of at most 0.0037.
Values may be sent and summed in bfloat16 or wider, within the bound.
No kernel may reach another device: no remote copies, remote signals or barrier semaphores. Data moves between devices by JAX's collectives and lax.ppermute only.
A program may use at most 128 MiB of HBM per device.

v0:
```python
import math

import jax
import jax.numpy as jnp
from jax import lax
from jax.sharding import PartitionSpec as P

HD = 128
SLAB = 128
SPAN = 2


def from_partner(x, axis, apart):
    return lax.ppermute(x, axis, [(i, i ^ 1 << apart) for i in range(lax.axis_size(axis))])


def select_slabs(source_rows, chosen):
    feature_width = source_rows.shape[1]
    slab_rows = source_rows.reshape(-1, SLAB, feature_width)
    picked = jnp.take(slab_rows, jnp.maximum(chosen, 0), axis=0)
    picked = jnp.where((chosen >= 0)[:, None, None], picked, jnp.zeros((), source_rows.dtype))
    return picked.reshape(-1, feature_width)


def attend_local(query_rows, key_rows, value_rows, key_count, positions):
    query_count, feature_width = query_rows.shape
    key_total = key_rows.shape[0]
    head_count = feature_width // HD
    group_heads = math.gcd(head_count, 4)
    columns = group_heads * HD
    key_valid = jnp.arange(key_total) < key_count

    def head_step(block_index, output_acc):
        start = block_index * columns
        query_part = lax.dynamic_slice_in_dim(query_rows, start, columns, 1).reshape(
            query_count, group_heads, HD
        )
        key_part = lax.dynamic_slice_in_dim(key_rows, start, columns, 1).reshape(
            key_total, group_heads, HD
        )
        value_part = lax.dynamic_slice_in_dim(value_rows, start, columns, 1).reshape(
            key_total, group_heads, HD
        )
        scores = jnp.einsum(
            "rhd,khd->hrk", query_part, key_part, preferred_element_type=jnp.float32
        ) * (1.0 / math.sqrt(HD))
        scores = jnp.where(key_valid[None, None, :], scores, -jnp.inf)
        peak = jnp.max(scores, axis=-1, keepdims=True)
        weights = jnp.exp(scores - peak)
        totals = jnp.sum(weights, axis=-1)
        mixed = jnp.einsum(
            "hrk,khd->rhd",
            weights.astype(jnp.bfloat16),
            value_part,
            preferred_element_type=jnp.float32,
        )
        mixed = mixed / jnp.transpose(totals)[:, :, None]
        return lax.dynamic_update_slice_in_dim(
            output_acc, mixed.reshape(query_count, columns), start, 1
        )

    result = lax.fori_loop(
        0,
        head_count // group_heads,
        head_step,
        jnp.zeros((query_count, feature_width), jnp.float32),
    )
    result = jnp.where((positions < key_count)[:, None], result, 0.0)
    return result.astype(jnp.bfloat16)


def local(queries, keys, values, lengths, help_table):
    row_count, feature_width = queries.shape
    device_index = lax.axis_index("seq")
    cand_count = lengths.shape[0]
    home_cand = device_index // SPAN
    cand_ids = jnp.arange(cand_count)
    home_length = jnp.sum(jnp.where(cand_ids == home_cand, lengths, 0))
    place = device_index % SPAN
    gathered_keys = keys
    gathered_values = values
    other_keys, other_values = from_partner((gathered_keys, gathered_values), "seq", 0)
    is_lower = device_index // 2**0 % 2 == 0
    gathered_keys = jnp.where(
        is_lower,
        jnp.concatenate([gathered_keys, other_keys], axis=0),
        jnp.concatenate([other_keys, gathered_keys], axis=0),
    )
    gathered_values = jnp.where(
        is_lower,
        jnp.concatenate([gathered_values, other_values], axis=0),
        jnp.concatenate([other_values, gathered_values], axis=0),
    )
    pair_bit = lax.axis_size("seq").bit_length() - 2
    partner_table = from_partner(help_table, "seq", pair_bit)
    partner_row = partner_table[0]
    slab_total = row_count // SLAB
    listed = jnp.any(partner_row[:, None] == jnp.arange(slab_total)[None, :], axis=0)
    home_positions = place * row_count + jnp.arange(row_count)
    home_full = attend_local(queries, gathered_keys, gathered_values, home_length, home_positions)
    attended = jnp.where(
        listed[:, None, None],
        jnp.zeros((), jnp.bfloat16),
        home_full.reshape(slab_total, SLAB, feature_width),
    )
    attended = attended.reshape(row_count, feature_width)
    helped = from_partner(select_slabs(home_full, partner_row), "seq", pair_bit)
    return (attended, helped)


def solution(mesh):
    return jax.shard_map(
        local,
        mesh=mesh,
        in_specs=(
            P(("groups", "seq"), None),
            P(("groups", "seq"), None),
            P(("groups", "seq"), None),
            P("groups"),
            P(("groups", "seq"), None),
        ),
        out_specs=(P(("groups", "seq"), None), P(("groups", "seq"), None)),
        check_vma=False,
    )
```

profile of v0, /device:TPU:0, one launch (start us, length us, event | category | flops | bytes accessed | tf_op | source)
XLA Modules:
  0.0 276.5 jit_solution(6617043448904739865)
XLA Ops:
  0.6 6.3 %copy.27 = bf16[768,2560]{0,1:T(8,128)(2,1)} copy(bf16[768,2560]{1,0:T(8,128)(2,1)} %param.8) | data formatting | bytes 7864320 | tf_op args[1]
  7.4 6.3 %copy.24 = bf16[768,2560]{0,1:T(8,128)(2,1)} copy(bf16[768,2560]{1,0:T(8,128)(2,1)} %param.9) | data formatting | bytes 7864320 | tf_op args[2]
  13.7 4.0 %collective-permute-start = (s32[1,2]{1,0:T(1,128)S(1)}, s32[1,2]{1,0:T(1,128)S(1)}, u32[]{:S(2)}, u32[]{:S(2)}) collective-permute-start(s32[1,2]{1,0:T(1,128)S(1)} %copy-done.3), channel_id=1, source_target_pairs={{0,8},{1,9},{2,10},{3,11},{4,12},{5,13},{6,14},{7,15},{8,0},{9,1},... | collective-permute-start | bytes 32 | tf_op jit(solution)/shard_map/ppermute | solution.py:14
  17.7 0.7 fusion.13
  19.5 10.7 %maximum_select_fusion.1 = bf16[1536,2560]{0,1:T(8,128)(2,1)} fusion(bf16[768,2560]{0,1:T(8,128)(2,1)} %collective-permute-done.2, bf16[768,2560]{0,1:T(8,128)(2,1)} %copy.27, pred[]{:T(512)S(6)} %eq.33), kind=kLoop, calls=%fused_computation.18 | loop fusion | flops 35389440 | bytes 15728641 | tf_op jit(solution)/shard_map/jit(_where)/select_n | solution.py:84
  30.2 7.9 %maximum_select_fusion = bf16[1536,2560]{0,1:T(8,128)(2,1)} fusion(bf16[768,2560]{0,1:T(8,128)(2,1)} %collective-permute-done.1, bf16[768,2560]{0,1:T(8,128)(2,1)S(1)} %copy-done.1, pred[]{:T(512)S(6)} %eq.33), kind=kLoop, calls=%fused_computation.17 | loop fusion | flops 35389440 | bytes 15728641 | tf_op jit(solution)/shard_map/jit(_where)/select_n | solution.py:89
  38.1 2.2 broadcast_in_dim.106.clone2
  40.2 167.5 %while.14 = (s32[]{:T(128)}, bf16[768,2560]{1,0:T(8,128)(2,1)}, bf16[1536,2560]{0,1:T(8,128)(2,1)}, bf16[768,2560]{1,0:T(8,128)(2,1)}, bf16[1536,2560]{0,1:T(8,1...) while((s32[]{:T(128)}, bf16[768,2560]{1,0:T(8,128)(2,1)}, ...), condition=%wide.region_5.6_spmd.clone, body=%wide.region_2.5_spmd.clone.sunk | while | flops 2468605440 | bytes 80283832 | solution.py:62
  40.3 3.2 %constant_dynamic-slice_fusion.5 = (bf16[1536,512]{0,1:T(8,128)(2,1)S(1)}, bf16[1536,512]{0,1:T(8,128)(2,1)}) fusion(bf16[1536,2560]{0,1:T(8,128)(2,1)} %get-tuple-element.236, s32[]{:T(128)S(6)} %select_n.115, bf16[1536,2560]{0,1:T(8,128)(2,1)} %get-tuple-element.234), kind=kLoop, calls=%fused_computation.12.clone.1 | loop fusion | bytes 6291460 | tf_op jit(solution)/shard_map/while/body/eval_jaxpr/dynamic_slice | solution.py:38
  43.5 1.2 constant_dynamic-slice_fusion.6
  44.9 0.6 iota_compare_fusion.2
  45.6 8.0 %fusion.27 = (f32[4,768]{1,0:T(4,128)S(1)}, f32[4,768,1536]{2,1,0:T(8,128)}) fusion(pred[1536]{0:T(1024)(128)(4,1)S(1)} %iota_compare_fusion.2, bf16[768,4,128]{0,2,1:T(8,128)(2,1)S(1)} %bitcast.45, bf16[1536,4,128]{0,2,1:T(8,128)(2,1)S(1)} %bitcast.44), kind=kOutput, calls=%fused_computation.4.clone.1 | convolution fusion | flops 1222112256 | bytes 21247488 | tf_op jit(solution)/shard_map/while/body/eval_jaxpr/rhd,khd->hrk/dot_general | solution.py:44
  53.6 10.3 %fusion.28 = f32[4,768]{1,0:T(4,128)S(1)} fusion(f32[4,768,1536]{2,1,0:T(8,128)} %get-tuple-element.210, f32[4,768]{1,0:T(4,128)S(1)} %get-tuple-element.211, pred[1536]{0:T(1024)(128)(4,1)S(1)} %iota_compare_fusion.2), kind=kLoop, calls=%fused_computation.5.clone.1 | loop fusion | flops 18871296 | bytes 18900480 | tf_op jit(solution)/shard_map/while/body/eval_jaxpr/reduce_sum | solution.py:50
  63.9 8.7 %bitcast_divide_fusion.2 = bf16[768,4,128]{0,2,1:T(8,128)(2,1)S(1)} fusion(bf16[1536,4,128]{0,2,1:T(8,128)(2,1)S(1)} %bitcast.46, f32[4,768,1536]{2,1,0:T(8,128)} %get-tuple-element.210, f32[4,768]{1,0:T(4,128)S(1)} %get-tuple-element.211, pred[1536]{0:T(1024)(128)(4,1)S(1)} %iota_compare_fusion.2, f32[768,4]{0,1:T(4,128)S(1)} %bitcast.49), kind=kOutput, calls=%fused_computation.9.clone.1 | convolution fusion | flops 1227620352 | bytes 21259776 | tf_op jit(solution)/shard_map/while/body/eval_jaxpr/hrk,khd->rhd/dot_general | solution.py:51
  72.8 0.9 constant_dynamic-update-slice_fusion.2
  73.7 3.2 %constant_dynamic-slice_fusion.5 = (bf16[1536,512]{0,1:T(8,128)(2,1)S(1)}, bf16[1536,512]{0,1:T(8,128)(2,1)}) fusion(bf16[1536,2560]{0,1:T(8,128)(2,1)} %get-tuple-element.236, s32[]{:T(128)S(6)} %select_n.115, bf16[1536,2560]{0,1:T(8,128)(2,1)} %get-tuple-element.234), kind=kLoop, calls=%fused_computation.12.clone.1 | loop fusion | bytes 6291460 | tf_op jit(solution)/shard_map/while/body/eval_jaxpr/dynamic_slice | solution.py:38
  77.0 1.2 constant_dynamic-slice_fusion.6
  78.4 0.6 iota_compare_fusion.2
  79.1 8.0 %fusion.27 = (f32[4,768]{1,0:T(4,128)S(1)}, f32[4,768,1536]{2,1,0:T(8,128)}) fusion(pred[1536]{0:T(1024)(128)(4,1)S(1)} %iota_compare_fusion.2, bf16[768,4,128]{0,2,1:T(8,128)(2,1)S(1)} %bitcast.45, bf16[1536,4,128]{0,2,1:T(8,128)(2,1)S(1)} %bitcast.44), kind=kOutput, calls=%fused_computation.4.clone.1 | convolution fusion | flops 1222112256 | bytes 21247488 | tf_op jit(solution)/shard_map/while/body/eval_jaxpr/rhd,khd->hrk/dot_general | solution.py:44
  87.1 10.3 %fusion.28 = f32[4,768]{1,0:T(4,128)S(1)} fusion(f32[4,768,1536]{2,1,0:T(8,128)} %get-tuple-element.210, f32[4,768]{1,0:T(4,128)S(1)} %get-tuple-element.211, pred[1536]{0:T(1024)(128)(4,1)S(1)} %iota_compare_fusion.2), kind=kLoop, calls=%fused_computation.5.clone.1 | loop fusion | flops 18871296 | bytes 18900480 | tf_op jit(solution)/shard_map/while/body/eval_jaxpr/reduce_sum | solution.py:50
  97.4 8.7 %bitcast_divide_fusion.2 = bf16[768,4,128]{0,2,1:T(8,128)(2,1)S(1)} fusion(bf16[1536,4,128]{0,2,1:T(8,128)(2,1)S(1)} %bitcast.46, f32[4,768,1536]{2,1,0:T(8,128)} %get-tuple-element.210, f32[4,768]{1,0:T(4,128)S(1)} %get-tuple-element.211, pred[1536]{0:T(1024)(128)(4,1)S(1)} %iota_compare_fusion.2, f32[768,4]{0,1:T(4,128)S(1)} %bitcast.49), kind=kOutput, calls=%fused_computation.9.clone.1 | convolution fusion | flops 1227620352 | bytes 21259776 | tf_op jit(solution)/shard_map/while/body/eval_jaxpr/hrk,khd->rhd/dot_general | solution.py:51
  106.3 0.9 constant_dynamic-update-slice_fusion.2
  107.2 3.2 %constant_dynamic-slice_fusion.5 = (bf16[1536,512]{0,1:T(8,128)(2,1)S(1)}, bf16[1536,512]{0,1:T(8,128)(2,1)}) fusion(bf16[1536,2560]{0,1:T(8,128)(2,1)} %get-tuple-element.236, s32[]{:T(128)S(6)} %select_n.115, bf16[1536,2560]{0,1:T(8,128)(2,1)} %get-tuple-element.234), kind=kLoop, calls=%fused_computation.12.clone.1 | loop fusion | bytes 6291460 | tf_op jit(solution)/shard_map/while/body/eval_jaxpr/dynamic_slice | solution.py:38
  110.5 1.2 constant_dynamic-slice_fusion.6
  111.9 0.6 iota_compare_fusion.2
  112.6 8.0 %fusion.27 = (f32[4,768]{1,0:T(4,128)S(1)}, f32[4,768,1536]{2,1,0:T(8,128)}) fusion(pred[1536]{0:T(1024)(128)(4,1)S(1)} %iota_compare_fusion.2, bf16[768,4,128]{0,2,1:T(8,128)(2,1)S(1)} %bitcast.45, bf16[1536,4,128]{0,2,1:T(8,128)(2,1)S(1)} %bitcast.44), kind=kOutput, calls=%fused_computation.4.clone.1 | convolution fusion | flops 1222112256 | bytes 21247488 | tf_op jit(solution)/shard_map/while/body/eval_jaxpr/rhd,khd->hrk/dot_general | solution.py:44
  120.6 10.3 %fusion.28 = f32[4,768]{1,0:T(4,128)S(1)} fusion(f32[4,768,1536]{2,1,0:T(8,128)} %get-tuple-element.210, f32[4,768]{1,0:T(4,128)S(1)} %get-tuple-element.211, pred[1536]{0:T(1024)(128)(4,1)S(1)} %iota_compare_fusion.2), kind=kLoop, calls=%fused_computation.5.clone.1 | loop fusion | flops 18871296 | bytes 18900480 | tf_op jit(solution)/shard_map/while/body/eval_jaxpr/reduce_sum | solution.py:50
  130.8 8.7 %bitcast_divide_fusion.2 = bf16[768,4,128]{0,2,1:T(8,128)(2,1)S(1)} fusion(bf16[1536,4,128]{0,2,1:T(8,128)(2,1)S(1)} %bitcast.46, f32[4,768,1536]{2,1,0:T(8,128)} %get-tuple-element.210, f32[4,768]{1,0:T(4,128)S(1)} %get-tuple-element.211, pred[1536]{0:T(1024)(128)(4,1)S(1)} %iota_compare_fusion.2, f32[768,4]{0,1:T(4,128)S(1)} %bitcast.49), kind=kOutput, calls=%fused_computation.9.clone.1 | convolution fusion | flops 1227620352 | bytes 21259776 | tf_op jit(solution)/shard_map/while/body/eval_jaxpr/hrk,khd->rhd/dot_general | solution.py:51
  139.8 0.9 constant_dynamic-update-slice_fusion.2
  140.7 3.2 %constant_dynamic-slice_fusion.5 = (bf16[1536,512]{0,1:T(8,128)(2,1)S(1)}, bf16[1536,512]{0,1:T(8,128)(2,1)}) fusion(bf16[1536,2560]{0,1:T(8,128)(2,1)} %get-tuple-element.236, s32[]{:T(128)S(6)} %select_n.115, bf16[1536,2560]{0,1:T(8,128)(2,1)} %get-tuple-element.234), kind=kLoop, calls=%fused_computation.12.clone.1 | loop fusion | bytes 6291460 | tf_op jit(solution)/shard_map/while/body/eval_jaxpr/dynamic_slice | solution.py:38
  144.0 1.2 constant_dynamic-slice_fusion.6
  145.4 0.6 iota_compare_fusion.2
  146.1 8.0 %fusion.27 = (f32[4,768]{1,0:T(4,128)S(1)}, f32[4,768,1536]{2,1,0:T(8,128)}) fusion(pred[1536]{0:T(1024)(128)(4,1)S(1)} %iota_compare_fusion.2, bf16[768,4,128]{0,2,1:T(8,128)(2,1)S(1)} %bitcast.45, bf16[1536,4,128]{0,2,1:T(8,128)(2,1)S(1)} %bitcast.44), kind=kOutput, calls=%fused_computation.4.clone.1 | convolution fusion | flops 1222112256 | bytes 21247488 | tf_op jit(solution)/shard_map/while/body/eval_jaxpr/rhd,khd->hrk/dot_general | solution.py:44
  154.0 10.3 %fusion.28 = f32[4,768]{1,0:T(4,128)S(1)} fusion(f32[4,768,1536]{2,1,0:T(8,128)} %get-tuple-element.210, f32[4,768]{1,0:T(4,128)S(1)} %get-tuple-element.211, pred[1536]{0:T(1024)(128)(4,1)S(1)} %iota_compare_fusion.2), kind=kLoop, calls=%fused_computation.5.clone.1 | loop fusion | flops 18871296 | bytes 18900480 | tf_op jit(solution)/shard_map/while/body/eval_jaxpr/reduce_sum | solution.py:50
  164.3 8.7 %bitcast_divide_fusion.2 = bf16[768,4,128]{0,2,1:T(8,128)(2,1)S(1)} fusion(bf16[1536,4,128]{0,2,1:T(8,128)(2,1)S(1)} %bitcast.46, f32[4,768,1536]{2,1,0:T(8,128)} %get-tuple-element.210, f32[4,768]{1,0:T(4,128)S(1)} %get-tuple-element.211, pred[1536]{0:T(1024)(128)(4,1)S(1)} %iota_compare_fusion.2, f32[768,4]{0,1:T(4,128)S(1)} %bitcast.49), kind=kOutput, calls=%fused_computation.9.clone.1 | convolution fusion | flops 1227620352 | bytes 21259776 | tf_op jit(solution)/shard_map/while/body/eval_jaxpr/hrk,khd->rhd/dot_general | solution.py:51
  173.3 0.9 constant_dynamic-update-slice_fusion.2
  174.2 3.2 %constant_dynamic-slice_fusion.5 = (bf16[1536,512]{0,1:T(8,128)(2,1)S(1)}, bf16[1536,512]{0,1:T(8,128)(2,1)}) fusion(bf16[1536,2560]{0,1:T(8,128)(2,1)} %get-tuple-element.236, s32[]{:T(128)S(6)} %select_n.115, bf16[1536,2560]{0,1:T(8,128)(2,1)} %get-tuple-element.234), kind=kLoop, calls=%fused_computation.12.clone.1 | loop fusion | bytes 6291460 | tf_op jit(solution)/shard_map/while/body/eval_jaxpr/dynamic_slice | solution.py:38
  177.4 1.2 constant_dynamic-slice_fusion.6
  178.9 0.6 iota_compare_fusion.2
  179.6 8.0 %fusion.27 = (f32[4,768]{1,0:T(4,128)S(1)}, f32[4,768,1536]{2,1,0:T(8,128)}) fusion(pred[1536]{0:T(1024)(128)(4,1)S(1)} %iota_compare_fusion.2, bf16[768,4,128]{0,2,1:T(8,128)(2,1)S(1)} %bitcast.45, bf16[1536,4,128]{0,2,1:T(8,128)(2,1)S(1)} %bitcast.44), kind=kOutput, calls=%fused_computation.4.clone.1 | convolution fusion | flops 1222112256 | bytes 21247488 | tf_op jit(solution)/shard_map/while/body/eval_jaxpr/rhd,khd->hrk/dot_general | solution.py:44
  187.5 10.3 %fusion.28 = f32[4,768]{1,0:T(4,128)S(1)} fusion(f32[4,768,1536]{2,1,0:T(8,128)} %get-tuple-element.210, f32[4,768]{1,0:T(4,128)S(1)} %get-tuple-element.211, pred[1536]{0:T(1024)(128)(4,1)S(1)} %iota_compare_fusion.2), kind=kLoop, calls=%fused_computation.5.clone.1 | loop fusion | flops 18871296 | bytes 18900480 | tf_op jit(solution)/shard_map/while/body/eval_jaxpr/reduce_sum | solution.py:50
  197.8 8.7 %bitcast_divide_fusion.2 = bf16[768,4,128]{0,2,1:T(8,128)(2,1)S(1)} fusion(bf16[1536,4,128]{0,2,1:T(8,128)(2,1)S(1)} %bitcast.46, f32[4,768,1536]{2,1,0:T(8,128)} %get-tuple-element.210, f32[4,768]{1,0:T(4,128)S(1)} %get-tuple-element.211, pred[1536]{0:T(1024)(128)(4,1)S(1)} %iota_compare_fusion.2, f32[768,4]{0,1:T(4,128)S(1)} %bitcast.49), kind=kOutput, calls=%fused_computation.9.clone.1 | convolution fusion | flops 1227620352 | bytes 21259776 | tf_op jit(solution)/shard_map/while/body/eval_jaxpr/hrk,khd->rhd/dot_general | solution.py:51
  206.8 0.9 constant_dynamic-update-slice_fusion.2
  207.7 5.4 %broadcast_select_fusion = (bf16[768,2560]{1,0:T(8,128)(2,1)}, bf16[768,2560]{1,0:T(8,128)(2,1)}) fusion(pred[768]{0:T(1024)(128)(4,1)S(1)} %broadcast_bitcast_fusion, bf16[768,2560]{1,0:T(8,128)(2,1)} %get-tuple-element.111, pred[768]{0:T(1024)(128)(4,1)S(1)} %add_compare_fusion), kind=kLoop, calls=%fused_computation.20 | loop fusion | flops 3932160 | bytes 11798016 | tf_op jit(solution)/shard_map/jit(_where)/select_n | solution.py:101
  213.1 2.7 gather_fusion
  216.2 3.0 %collective-permute-start.3 = (bf16[256,2560]{1,0:T(8,128)(2,1)S(1)}, bf16[256,2560]{1,0:T(8,128)(2,1)S(1)}, u32[]{:S(2)}, u32[]{:S(2)}) collective-permute-start(bf16[256,2560]{1,0:T(8,128)(2,1)S(1)} %fusion.12), channel_id=1, source_target_pairs={{0,8},{1,9},{2,10},{3,11},{4,12},{5,13},{6,14},{7,15},{8,0},{9,1},... | collective-permute-start | bytes 3932168 | tf_op jit(solution)/shard_map/ppermute | solution.py:14
  219.2 56.3 %collective-permute-done.3 = bf16[256,2560]{1,0:T(8,128)(2,1)S(1)} collective-permute-done((bf16[256,2560]{1,0:T(8,128)(2,1)S(1)}, bf16[256,2560]{1,0:T(8,128)(2,1)S(1)}, u32[]{:S(2)}, u32[]{:S(2)}) %collective-permute-start.3) | collective-permute-done | bytes 1310752 | tf_op jit(solution)/shard_map/ppermute | solution.py:14
  275.5 1.1 copy.49
  (39 shorter events, 4.7 us)
Async XLA Ops:
  6.9 6.8 %copy-start.3 = (s32[1,2]{1,0:T(1,128)S(1)}, s32[1,2]{1,0:T(1,128)}, u32[]{:S(2)}) copy-start(s32[1,2]{1,0:T(1,128)} %param.11) | copy-start | bytes 28
  6.9 10.8 %copy-start.2 = (s32[8]{0:T(128)S(1)}, s32[8]{0:T(128)}, u32[]{:S(2)}) copy-start(s32[8]{0:T(128)} %param.10) | copy-start | bytes 100
  6.9 12.6 %collective-permute-start.2 = (bf16[768,2560]{0,1:T(8,128)(2,1)}, bf16[768,2560]{0,1:T(8,128)(2,1)}, u32[]{:S(2)}, u32[]{:S(2)}) collective-permute-start(bf16[768,2560]{0,1:T(8,128)(2,1)} %copy.27), channel_id=1, source_target_pairs={{0,1},{1,0},{2,3},{3,2},{4,5},{5,4},{6,7},{7,6},{8,9},{9,8},{10,11... | collective-permute-start | bytes 11796488 | tf_op jit(solution)/shard_map/ppermute | solution.py:14
  13.6 16.5 %collective-permute-start.1 = (bf16[768,2560]{0,1:T(8,128)(2,1)}, bf16[768,2560]{0,1:T(8,128)(2,1)}, u32[]{:S(2)}, u32[]{:S(2)}) collective-permute-start(bf16[768,2560]{0,1:T(8,128)(2,1)} %copy.24), channel_id=1, source_target_pairs={{0,1},{1,0},{2,3},{3,2},{4,5},{5,4},{6,7},{7,6},{8,9},{9,8},{10,11... | collective-permute-start | bytes 11796488 | tf_op jit(solution)/shard_map/ppermute | solution.py:14
  13.7 5.6 %collective-permute-start = (s32[1,2]{1,0:T(1,128)S(1)}, s32[1,2]{1,0:T(1,128)S(1)}, u32[]{:S(2)}, u32[]{:S(2)}) collective-permute-start(s32[1,2]{1,0:T(1,128)S(1)} %copy-done.3), channel_id=1, source_target_pairs={{0,8},{1,9},{2,10},{3,11},{4,12},{5,13},{6,14},{7,15},{8,0},{9,1},... | collective-permute-start | bytes 32 | tf_op jit(solution)/shard_map/ppermute | solution.py:14
  19.5 10.7 %copy-start.1 = (bf16[768,2560]{0,1:T(8,128)(2,1)S(1)}, bf16[768,2560]{0,1:T(8,128)(2,1)}, u32[]{:S(2)}) copy-start(bf16[768,2560]{0,1:T(8,128)(2,1)} %copy.24) | copy-start | bytes 11796484
  53.6 10.3 %copy-start = (bf16[1536,512]{0,1:T(8,128)(2,1)S(1)}, bf16[1536,512]{0,1:T(8,128)(2,1)}, u32[]{:S(2)}) copy-start(bf16[1536,512]{0,1:T(8,128)(2,1)} %get-tuple-element.208) | copy-start | bytes 4718596 | tf_op jit(solution)/shard_map/while
  87.1 10.3 %copy-start = (bf16[1536,512]{0,1:T(8,128)(2,1)S(1)}, bf16[1536,512]{0,1:T(8,128)(2,1)}, u32[]{:S(2)}) copy-start(bf16[1536,512]{0,1:T(8,128)(2,1)} %get-tuple-element.208) | copy-start | bytes 4718596 | tf_op jit(solution)/shard_map/while
  120.6 10.3 %copy-start = (bf16[1536,512]{0,1:T(8,128)(2,1)S(1)}, bf16[1536,512]{0,1:T(8,128)(2,1)}, u32[]{:S(2)}) copy-start(bf16[1536,512]{0,1:T(8,128)(2,1)} %get-tuple-element.208) | copy-start | bytes 4718596 | tf_op jit(solution)/shard_map/while
  154.0 10.3 %copy-start = (bf16[1536,512]{0,1:T(8,128)(2,1)S(1)}, bf16[1536,512]{0,1:T(8,128)(2,1)}, u32[]{:S(2)}) copy-start(bf16[1536,512]{0,1:T(8,128)(2,1)} %get-tuple-element.208) | copy-start | bytes 4718596 | tf_op jit(solution)/shard_map/while
  187.5 10.3 %copy-start = (bf16[1536,512]{0,1:T(8,128)(2,1)S(1)}, bf16[1536,512]{0,1:T(8,128)(2,1)}, u32[]{:S(2)}) copy-start(bf16[1536,512]{0,1:T(8,128)(2,1)} %get-tuple-element.208) | copy-start | bytes 4718596 | tf_op jit(solution)/shard_map/while
  216.2 59.3 %collective-permute-start.3 = (bf16[256,2560]{1,0:T(8,128)(2,1)S(1)}, bf16[256,2560]{1,0:T(8,128)(2,1)S(1)}, u32[]{:S(2)}, u32[]{:S(2)}) collective-permute-start(bf16[256,2560]{1,0:T(8,128)(2,1)S(1)} %fusion.12), channel_id=1, source_target_pairs={{0,8},{1,9},{2,10},{3,11},{4,12},{5,13},{6,14},{7,15},{8,0},{9,1},... | collective-permute-start | bytes 3932168 | tf_op jit(solution)/shard_map/ppermute | solution.py:14
where the time goes:
time: 277 us
  matrix products  83.2 us (30%)
  other arithmetic  80.3 us (29%)
  waiting for transfers between devices  56.5 us (20%)
  local copies, waits for them, and re-layouts  48.2 us (17%)
  starting transfers between devices  7.53 us (3%)
    ppermute x4, waiting for transfers between devices, from_partner(): lax.ppermute(x, axis, [(i, i ^ 1 << apart) for i in range(lax.axis_size(a...  56.5 us
    reduce_sum x5, other arithmetic, head_step(): totals = jnp.sum(weights, axis=-1)  51.4 us
    dot_general x5, matrix products, head_step(): jnp.einsum('hrk,khd->rhd', weights.astype(jnp.bfloat16), value_part, pref...  43.3 us
    dot_general x5, matrix products, head_step(): jnp.einsum('rhd,khd->hrk', query_part, key_part, preferred_element_type=j...  39.9 us
    dynamic_slice x5, local copies, waits for them, and re-layouts, head_step(): lax.dynamic_slice_in_dim(key_rows, start, columns, 1)  16.1 us
    unnamed x9, local copies, waits for them, and re-layouts  13.6 us
    select_n x1, other arithmetic, local(): jnp.where(is_lower, jnp.concatenate([gathered_keys, other_keys], axis=0),...  10.7 us
    select_n x1, other arithmetic, local(): jnp.where(is_lower, jnp.concatenate([gathered_values, other_values], axis...  7.89 us
  transfers between devices with their start and end apart: 4, of which 2 were waited for; matrix products, arithmetic and copies ran while one was open for 7% of the time, Pallas kernels for 0%

commit v1 on v0

v1 whole, which is shorter than its diff:
```python
import math

import jax
import jax.numpy as jnp
from jax import lax
from jax.experimental import pallas as pl
from jax.experimental.pallas import tpu as pltpu
from jax.sharding import PartitionSpec as P

HD = 128
SLAB = 128
SPAN = 2
KEY_TILE = 256
ROW_CHUNK = 16
STEP_HEADS = 2
WIDTH = STEP_HEADS * HD
SCALE = math.log2(math.e) / math.sqrt(HD)
CHUNK_HEADS = (4, 6, 10)


def rows_of(start):
    return pl.ds(pl.multiple_of(start, SLAB), SLAB)


def scaled_queries(ref, slabs, columns):
    wide = jnp.concatenate([ref[rows_of(s * SLAB), columns] for s in slabs], axis=0)
    wide = wide.astype(jnp.float32) * SCALE
    high = wide.astype(jnp.bfloat16)
    low = (wide - high.astype(jnp.float32)).astype(jnp.bfloat16)
    return jnp.concatenate([high, low], axis=1)


def key_tile(ref, start, columns, limit):
    tile = ref[pl.ds(start, KEY_TILE), columns]
    if limit is not None:
        first = ref[pl.ds(0, 16), columns].astype(jnp.float32)[0:1]
        valid = lax.broadcasted_iota(jnp.int32, tile.shape, 0) + start < limit
        tile = jnp.where(valid, tile.astype(jnp.float32), first).astype(jnp.bfloat16)
    return jnp.concatenate([tile, tile], axis=1)


def value_tile(ref, start, columns, limit):
    tile = ref[pl.ds(start, KEY_TILE), columns]
    ones = jnp.ones(tile.shape, jnp.bfloat16)
    if limit is not None:
        valid = lax.broadcasted_iota(jnp.int32, tile.shape, 0) + start < limit
        tile = jnp.where(valid, tile.astype(jnp.float32), 0.0).astype(jnp.bfloat16)
        ones = jnp.where(valid, 1.0, 0.0).astype(jnp.bfloat16)
    return jnp.concatenate([tile, ones], axis=1)


def attend(query_ref, pairs, mask_all, slab_sets, position, length, score_refs, weight_refs, store):
    tiles = []
    for key_ref, value_ref, limit in pairs:
        count = key_ref.shape[0] // KEY_TILE
        for t in range(count):
            masked = mask_all or t == count - 1
            tiles.append((key_ref, value_ref, t * KEY_TILE, limit if masked else None))
    total = len(tiles)
    keys = total * KEY_TILE
    items = [(h, slabs) for h in range(STEP_HEADS) for slabs in slab_sets]
    rows = SLAB * len(slab_sets[0])
    chunks = rows // ROW_CHUNK
    for t in range(len(items) + 2):
        now = items[t] if t < len(items) else None
        middle = 0 <= t - 1 < len(items)
        last = items[t - 2] if t >= 2 else None
        if now:
            now_columns = pl.ds(now[0] * HD, HD)
            scaled = scaled_queries(query_ref, now[1], now_columns)
        if last:
            last_columns = pl.ds(last[0] * HD, HD)
        mixed = None
        for j, (key_ref, value_ref, start, limit) in enumerate(tiles):
            if now:
                score_refs[t % 2][:rows, pl.ds(j * KEY_TILE, KEY_TILE)] = lax.dot_general(
                    scaled,
                    key_tile(key_ref, start, now_columns, limit),
                    (((1,), (1,)), ((), ())),
                    preferred_element_type=jnp.float32,
                )
            if last:
                part = jnp.dot(
                    weight_refs[t % 2][:rows, pl.ds(j * KEY_TILE, KEY_TILE)],
                    value_tile(value_ref, start, last_columns, limit),
                    preferred_element_type=jnp.float32,
                )
                mixed = part if mixed is None else mixed + part
            if middle:
                for c in range(j * chunks // total, (j + 1) * chunks // total):
                    here = pl.ds(c * ROW_CHUNK, ROW_CHUNK)
                    scores = score_refs[(t - 1) % 2][here, :keys]
                    peak = jnp.max(scores, axis=1, keepdims=True)
                    weight_refs[(t - 1) % 2][here, :keys] = jnp.exp2(scores - peak).astype(
                        jnp.bfloat16
                    )
        if last:
            result = mixed[:, :HD] / mixed[:, HD:]
            for n, slab in enumerate(last[1]):
                rows_at = position + slab * SLAB + lax.broadcasted_iota(jnp.int32, (SLAB, HD), 0)
                part = jnp.where(rows_at < length, result[n * SLAB : (n + 1) * SLAB], 0.0)
                store(last[0], n, slab, part.astype(jnp.bfloat16))


def limits(length, place, row_count):
    own = jnp.clip(length - place * row_count, 0, row_count)
    other = jnp.clip(length - (1 - place) * row_count, 0, row_count)
    return own, other


def help_body(me, lengths, listed, q, ko, vo, kx, vx, out, s0, s1, w0, w1):
    row_count = q.shape[0]
    length = lengths[me[0] // SPAN]
    place = me[0] % SPAN
    own, other = limits(length, place, row_count)
    active = listed[0, 0] >= 0

    @pl.when(active)
    def _():
        def store(h, n, slab, part):
            out[pl.ds(n * SLAB, SLAB), pl.ds(h * HD, HD)] = part

        attend(
            q, [(ko, vo, own), (kx, vx, other)], False, [[listed[0, 0], listed[0, 1]]],
            place * row_count, length, (s0, s1), (w0, w1), store,
        )

    @pl.when(jnp.logical_not(active))
    def _():
        out[...] = jnp.zeros_like(out)


def home_body(me, lengths, listed, q, ko, vo, kx, vx, *rest):
    out, s0, s1, w0, w1 = rest[-5:]
    row_count = q.shape[0]
    length = lengths[me[0] // SPAN]
    place = me[0] % SPAN
    own, other = limits(length, place, row_count)
    long = length > row_count
    low = jnp.minimum(listed[0, 0], listed[0, 1])
    high = jnp.maximum(listed[0, 0], listed[0, 1])

    def store(h, n, slab, part):
        out[rows_of(slab * SLAB), pl.ds(h * HD, HD)] = part

    @pl.when(long)
    def _():
        kept = []
        for n in range(row_count // SLAB - 2):
            slab = n + (n >= low).astype(jnp.int32)
            kept.append(slab + (slab >= high).astype(jnp.int32))
        half = len(kept) // 2
        attend(
            q, [(ko, vo, own), (kx, vx, other)], False, [kept[:half], kept[half:]],
            place * row_count, length, (s0, s1), (w0, w1), store,
        )
        for slab in (low, high):
            out[rows_of(slab * SLAB), :] = jnp.zeros((SLAB, WIDTH), jnp.bfloat16)

    @pl.when(jnp.logical_not(long) & (place == 0))
    def _():
        sets = [[n, n + 1] for n in range(0, row_count // SLAB, 2)]
        attend(q, [(ko, vo, own)], True, sets, 0, length, (s0, s1), (w0, w1), store)

    @pl.when(jnp.logical_not(long) & (place == 1))
    def _():
        out[...] = jnp.zeros_like(out)


def call(body, scalars, q, k, v, kx, vx, first, heads, rows, before=None):
    row_count, features = q.shape
    at = first // STEP_HEADS
    whole = pl.BlockSpec((row_count, WIDTH), lambda g, *_: (0, g + at))
    part = pl.BlockSpec((row_count, WIDTH), lambda g, *_: (0, g))
    in_specs = [whole, whole, whole, part, part]
    operands = [q, k, v, kx, vx]
    aliases = {}
    if rows == row_count:
        out_shape = jax.ShapeDtypeStruct((row_count, features), jnp.bfloat16)
        out_spec = whole
        if before is not None:
            in_specs.append(pl.BlockSpec(memory_space=pl.ANY))
            operands.append(before)
            aliases = {len(scalars) + 5: 0}
        worked = row_count - 2 * SLAB
    else:
        out_shape = jax.ShapeDtypeStruct((rows, heads * HD), jnp.bfloat16)
        out_spec = pl.BlockSpec((rows, WIDTH), lambda g, *_: (0, g))
        worked = rows
    item = 2 * SLAB
    scores = pltpu.VMEM((item, SPAN * row_count), jnp.float32)
    weights = pltpu.VMEM((item, SPAN * row_count), jnp.bfloat16)
    return pl.pallas_call(
        body,
        out_shape=out_shape,
        grid_spec=pltpu.PrefetchScalarGridSpec(
            num_scalar_prefetch=len(scalars),
            grid=(heads // STEP_HEADS,),
            in_specs=in_specs,
            out_specs=out_spec,
            scratch_shapes=[scores, scores, weights, weights],
        ),
        input_output_aliases=aliases,
        compiler_params=pltpu.CompilerParams(
            vmem_limit_bytes=40 << 20, dimension_semantics=("arbitrary",)
        ),
        cost_estimate=pl.CostEstimate(
            flops=8 * worked * SPAN * row_count * heads * HD,
            bytes_accessed=2 * 6 * row_count * heads * HD,
            transcendentals=worked * SPAN * row_count * heads,
        ),
    )(*scalars, *operands)


def local(queries, keys, values, lengths, help_table):
    row_count, features = queries.shape
    size = lax.axis_size("seq")
    core_pairs = [(i, i ^ 1) for i in range(size)]
    far_pairs = [(i, i ^ size // 2) for i in range(size)]
    listed = lax.ppermute(help_table, "seq", far_pairs)
    me = lax.axis_index("seq").astype(jnp.int32).reshape(1)
    scalars = (me, lengths, listed)

    edges = [0]
    for heads in CHUNK_HEADS:
        edges.append(edges[-1] + heads)
    assert edges[-1] * HD == features
    chunks = []
    for first, end in zip(edges[:-1], edges[1:]):
        part = (keys[:, first * HD : end * HD], values[:, first * HD : end * HD])
        chunks.append((first, end - first, lax.ppermute(part, "seq", core_pairs)))

    helped = []
    for first, heads, (kx, vx) in chunks:
        outputs = call(
            help_body, scalars, queries, keys, values, kx, vx, first, heads, help_table.shape[1] * SLAB
        )
        helped.append(lax.ppermute(outputs, "seq", far_pairs))
    attended = None
    for first, heads, (kx, vx) in chunks:
        attended = call(
            home_body, scalars, queries, keys, values, kx, vx, first, heads, row_count, attended
        )
    return attended, jnp.concatenate(helped, axis=1)


def solution(mesh):
    rows = P(("groups", "seq"), None)
    return jax.shard_map(
        local,
        mesh=mesh,
        in_specs=(rows, rows, rows, P("groups"), rows),
        out_specs=(rows, rows),
        check_vma=False,
    )
```

time: 277 us -> 90.7 us (0.33)
  matrix products: 83.2 us -> 0 us
  other arithmetic: 80.3 us -> 1.14 us
  Pallas kernels: 0 us -> 51.1 us
  waiting for transfers between devices: 56.5 us -> 15.4 us
  local copies, waits for them, and re-layouts: 48.2 us -> 16.6 us
    dot_general x10 -> x0, matrix products: 83.2 us -> none  [the longest x5 43.3 us: head_step(): jnp.einsum('hrk,khd->rhd', weights.astype(jnp.bfloat16), value_part, pref...]
    reduce_sum x6 -> x0, other arithmetic: 52.1 us -> none  [the longest x5 51.4 us: head_step(): totals = jnp.sum(weights, axis=-1)]
    pallas_call x0 -> x6, Pallas kernels: none -> 51.1 us  [call(): pl.pallas_call(body, out_shape=out_shape, grid_spec=pltpu.PrefetchScalarG...]
    ppermute x4 -> x10, waiting for transfers between devices: 56.5 us -> 15.4 us  [the longest x3 15.4 us: local(): helped.append(lax.ppermute(outputs, 'seq', far_pairs))]
    select_n x4 -> x0, other arithmetic: 24.3 us -> none  [the longest x1 10.7 us: local(): jnp.where(is_lower, jnp.concatenate([gathered_keys, other_keys], axis=0),...]
    dynamic_slice x15 -> x0, local copies, waits for them, and re-layouts: 23.4 us -> none  [the longest x5 16.1 us: head_step(): lax.dynamic_slice_in_dim(key_rows, start, columns, 1)]
    slice x0 -> x6, local copies, waits for them, and re-layouts: none -> 10.3 us  [local(): part = (keys[:, first * HD:end * HD], values[:, first * HD:end * HD])]
    unnamed x9 -> x12, local copies, waits for them, and re-layouts: 13.6 us -> 6.35 us
  transfers between devices with their start and end apart: 4 -> 10, of which waited for: 2 -> 1; matrix products, arithmetic and copies ran while one was open for 7% -> 10% of each run, Pallas kernels for 0% -> 56%
where the time goes in v1:
time: 90.7 us; the launch traced here: 90.9 us
  Pallas kernels  51.1 us (56%)
  local copies, waits for them, and re-layouts  16.6 us (18%)
  waiting for transfers between devices  15.4 us (17%)
  starting transfers between devices  5.95 us (7%)
  other arithmetic  1.14 us (1%)
    pallas_call x6, Pallas kernels, call(): pl.pallas_call(body, out_shape=out_shape, grid_spec=pltpu.PrefetchScalarG...  51.1 us
    ppermute x3, waiting for transfers between devices, local(): helped.append(lax.ppermute(outputs, 'seq', far_pairs))  15.4 us
    slice x6, local copies, waits for them, and re-layouts, local(): part = (keys[:, first * HD:end * HD], values[:, first * HD:end * HD])  10.3 us
    unnamed x12, local copies, waits for them, and re-layouts  6.35 us
    ppermute x1, starting transfers between devices, local(): listed = lax.ppermute(help_table, 'seq', far_pairs)  4.2 us
  transfers between devices with their start and end apart: 10, of which 1 were waited for; matrix products, arithmetic and copies ran while one was open for 10% of the time, Pallas kernels for 56%

profile of v1, /device:TPU:0, one launch (start us, length us, event | category | flops | bytes accessed | tf_op | source)
XLA Modules:
  0.0 90.9 jit_solution(7495798692434394755)
XLA Ops:
  0.6 1.2 %slice.23 = bf16[768,512]{1,0:T(8,128)(2,1)S(1)} slice(bf16[768,2560]{1,0:T(8,128)(2,1)} %vo.11), slice={[0:768], [0:512]} | slice | bytes 1572864 | tf_op jit(solution)/shard_map/slice | solution.py:230
  1.8 0.0 copy-start
  1.8 0.5 collective-permute-start.6
  2.3 3.2 %slice.19 = bf16[768,1280]{1,0:T(8,128)(2,1)} slice(bf16[768,2560]{1,0:T(8,128)(2,1)} %vo.11), slice={[0:768], [1280:2560]} | slice | bytes 3932160 | tf_op jit(solution)/shard_map/slice | solution.py:230
  5.6 0.0 copy-start.5
  5.6 0.0 collective-permute-start.2
  5.6 0.0 copy-done
  5.6 1.4 %slice.18 = bf16[768,1280]{1,0:T(8,128)(2,1)} slice(bf16[768,2560]{1,0:T(8,128)(2,1)S(1)} %copy-done), slice={[0:768], [1280:2560]} | slice | bytes 3932160 | tf_op jit(solution)/shard_map/slice | solution.py:230
  7.0 0.5 collective-permute-start.1
  7.5 0.9 %slice.22 = bf16[768,512]{1,0:T(8,128)(2,1)} slice(bf16[768,2560]{1,0:T(8,128)(2,1)S(1)} %copy-done), slice={[0:768], [0:512]} | slice | bytes 1572864 | tf_op jit(solution)/shard_map/slice | solution.py:230
  8.4 0.0 copy-start.4
  8.4 0.0 collective-permute-start.5
  8.4 0.0 copy-done.5
  8.4 4.2 %collective-permute-start = (s32[1,2]{1,0:T(1,128)S(1)}, s32[1,2]{1,0:T(1,128)S(1)}, u32[]{:S(2)}, u32[]{:S(2)}) collective-permute-start(s32[1,2]{1,0:T(1,128)S(1)} %copy-done.5), channel_id=1, source_target_pairs={{0,8},{1,9},{2,10},{3,11},{4,12},{5,13},{6,14},{7,15},{8,0},{9,1},... | collective-permute-start | bytes 32 | tf_op jit(solution)/shard_map/ppermute | solution.py:220
  12.6 1.1 %slice.20 = bf16[768,768]{1,0:T(8,128)(2,1)} slice(bf16[768,2560]{1,0:T(8,128)(2,1)S(1)} %copy-done), slice={[0:768], [512:1280]} | slice | bytes 2359296 | tf_op jit(solution)/shard_map/slice | solution.py:230
  13.7 2.4 %slice.21 = bf16[768,768]{1,0:T(8,128)(2,1)} slice(bf16[768,2560]{1,0:T(8,128)(2,1)} %vo.11), slice={[0:768], [512:1280]} | slice | bytes 2359296 | tf_op jit(solution)/shard_map/slice | solution.py:230
  16.1 0.0 collective-permute-done.listed
  16.2 0.0 collective-permute-start.4
  16.2 0.0 collective-permute-done.6.vx
  16.2 0.5 collective-permute-start.3
  16.7 0.0 collective-permute-done.5.kx
  16.7 0.0 copy-done.4
  16.7 0.0 copy-start.1
  16.7 2.1 %copy-done.1 = bf16[768,2560]{1,0:T(8,128)(2,1)S(1)} copy-done((bf16[768,2560]{1,0:T(8,128)(2,1)S(1)}, bf16[768,2560]{1,0:T(8,128)(2,1)}, u32[]{:S(2)}) %copy-start.1) | copy-done | bytes 3932184
  18.8 0.0 copy-start.2
  18.8 2.1 %copy-done.2 = bf16[768,2560]{1,0:T(8,128)(2,1)S(1)} copy-done((bf16[768,2560]{1,0:T(8,128)(2,1)S(1)}, bf16[768,2560]{1,0:T(8,128)(2,1)}, u32[]{:S(2)}) %copy-start.2) | copy-done | bytes 3932184
  20.9 0.0 copy-start.3
  20.9 2.1 %copy-done.3 = bf16[768,2560]{1,0:T(8,128)(2,1)S(1)} copy-done((bf16[768,2560]{1,0:T(8,128)(2,1)S(1)}, bf16[768,2560]{1,0:T(8,128)(2,1)}, u32[]{:S(2)}) %copy-start.3) | copy-done | bytes 3932184
  23.0 4.1 %shard_map.71 = bf16[256,512]{1,0:T(8,128)(2,1)S(1)} custom-call(s32[1]{0:T(128)} %bitcast.me, s32[8]{0:T(128)S(1)} %copy-done.4, s32[1,2]{1,0:T(1,128)S(1)} %collective-permute-done.listed, bf16[768,2560]{1,0:T(8,128)(2,1)S(1)} %copy-done.3, bf16[768,2560]{1,0:T(8,128)(2,1)S(1)} %copy-done.1, bf16[768,2560]{1,0:T(8,128)(2,1)S(1)} %copy-done.2, ...), custom_call_target="tpu_custom_call" | custom-call | flops 1610612736 | bytes 4718592 | tf_op jit(solution)/shard_map/pallas_call | solution.py:193
  27.1 0.1 collective-permute-start.7
  27.2 7.7 %shard_map.68.rest_0_ = bf16[768,2560]{1,0:T(8,128)(2,1)} custom-call(s32[1]{0:T(128)} %bitcast.me, s32[8]{0:T(128)S(1)} %copy-done.4, s32[1,2]{1,0:T(1,128)S(1)} %collective-permute-done.listed, bf16[768,2560]{1,0:T(8,128)(2,1)S(1)} %copy-done.3, bf16[768,2560]{1,0:T(8,128)(2,1)S(1)} %copy-done.1, bf16[768,2560]{1,0:T(8,128)(2,1)S(1)} %copy-done.2, ...), custom_call_target="tpu_custom_call" | custom-call | flops 3221225472 | bytes 4718592 | tf_op jit(solution)/shard_map/pallas_call | solution.py:193
  34.9 0.0 collective-permute-done.4.vx
  34.9 0.0 collective-permute-done.3.kx
  34.9 4.7 %shard_map.72 = bf16[256,768]{1,0:T(8,128)(2,1)S(1)} custom-call(s32[1]{0:T(128)} %bitcast.me, s32[8]{0:T(128)S(1)} %copy-done.4, s32[1,2]{1,0:T(1,128)S(1)} %collective-permute-done.listed, bf16[768,2560]{1,0:T(8,128)(2,1)S(1)} %copy-done.3, bf16[768,2560]{1,0:T(8,128)(2,1)S(1)} %copy-done.1, bf16[768,2560]{1,0:T(8,128)(2,1)S(1)} %copy-done.2, ...), custom_call_target="tpu_custom_call" | custom-call | flops 2415919104 | bytes 7077888 | tf_op jit(solution)/shard_map/pallas_call | solution.py:193
  39.6 0.1 collective-permute-start.8
  39.7 9.8 %shard_map.69.rest_0_ = bf16[768,2560]{1,0:T(8,128)(2,1)} custom-call(s32[1]{0:T(128)} %bitcast.me, s32[8]{0:T(128)S(1)} %copy-done.4, s32[1,2]{1,0:T(1,128)S(1)} %collective-permute-done.listed, bf16[768,2560]{1,0:T(8,128)(2,1)S(1)} %copy-done.3, bf16[768,2560]{1,0:T(8,128)(2,1)S(1)} %copy-done.1, ...), custom_call_target="tpu_custom_call", output_to_operand_aliasing={{}: (8, {})} | custom-call | flops 4831838208 | bytes 7077888 | tf_op jit(solution)/shard_map/pallas_call | solution.py:193
  49.5 0.0 collective-permute-done.2.vx
  49.5 0.0 collective-permute-done.1.kx
  49.5 8.5 %shard_map.73 = bf16[256,1280]{1,0:T(8,128)(2,1)S(1)} custom-call(s32[1]{0:T(128)} %bitcast.me, s32[8]{0:T(128)S(1)} %copy-done.4, s32[1,2]{1,0:T(1,128)S(1)} %collective-permute-done.listed, bf16[768,2560]{1,0:T(8,128)(2,1)S(1)} %copy-done.3, bf16[768,2560]{1,0:T(8,128)(2,1)S(1)} %copy-done.1, bf16[768,2560]{1,0:T(8,128)(2,1)} %vo.11, ...), custom_call_target="tpu_custom_call" | custom-call | flops 4026531840 | bytes 11796480 | tf_op jit(solution)/shard_map/pallas_call | solution.py:193
  58.0 0.1 collective-permute-start.9
  58.1 16.2 %shard_map.70 = bf16[768,2560]{1,0:T(8,128)(2,1)} custom-call(s32[1]{0:T(128)} %bitcast.me, s32[8]{0:T(128)S(1)} %copy-done.4, s32[1,2]{1,0:T(1,128)S(1)} %collective-permute-done.listed, bf16[768,2560]{1,0:T(8,128)(2,1)S(1)} %copy-done.3, bf16[768,2560]{1,0:T(8,128)(2,1)S(1)} %copy-done.1, bf16[768,2560]{1,0:T(8,128)(2,1)} %vo.11, ...), custom_call_target="tpu_custom_call", output_to_operand_aliasing={{}: (8, {})} | custom-call | flops 8053063680 | bytes 11796480 | tf_op jit(solution)/shard_map/pallas_call | solution.py:193
  74.3 0.0 collective-permute-done.7
  74.3 0.0 collective-permute-done.8
  74.4 15.4 %collective-permute-done.9 = bf16[256,1280]{1,0:T(8,128)(2,1)S(1)} collective-permute-done((bf16[256,1280]{1,0:T(8,128)(2,1)S(1)}, bf16[256,1280]{1,0:T(8,128)(2,1)S(1)}, u32[]{:S(2)}, u32[]{:S(2)}) %collective-permute-start.9) | collective-permute-done | bytes 655392 | tf_op jit(solution)/shard_map/ppermute | solution.py:238
  89.7 1.1 %pad_maximum_fusion = bf16[256,2560]{1,0:T(8,128)(2,1)} fusion(bf16[256,1280]{1,0:T(8,128)(2,1)S(1)} %collective-permute-done.9, bf16[256,768]{1,0:T(8,128)(2,1)S(1)} %collective-permute-done.8, bf16[256,512]{1,0:T(8,128)(2,1)S(1)} %collective-permute-done.7), kind=kLoop, calls=%fused_computation | loop fusion | flops 3932160 | bytes 2621440 | tf_op jit(solution)/shard_map/concatenate | solution.py:244
Async XLA Ops:
  1.8 3.8 %copy-start = (bf16[768,2560]{1,0:T(8,128)(2,1)S(1)}, bf16[768,2560]{1,0:T(8,128)(2,1)}, u32[]{:S(2)}) copy-start(bf16[768,2560]{1,0:T(8,128)(2,1)} %ko.11) | copy-start | bytes 11796484
  1.8 14.3 %collective-permute-start.6 = (bf16[768,512]{1,0:T(8,128)(2,1)S(1)}, bf16[768,512]{1,0:T(8,128)(2,1)S(1)}, u32[]{:S(2)}, u32[]{:S(2)}) collective-permute-start(bf16[768,512]{1,0:T(8,128)(2,1)S(1)} %slice.23), channel_id=1, source_target_pairs={{0,1},{1,0},{2,3},{3,2},{4,5},{5,4},{6,7},{7,6},{8,9},{9,8},{10,11... | collective-permute-start | bytes 2359304 | tf_op jit(solution)/shard_map/ppermute | solution.py:231
  5.6 2.9 %copy-start.5 = (s32[1,2]{1,0:T(1,128)S(1)}, s32[1,2]{1,0:T(1,128)}, u32[]{:S(2)}) copy-start(s32[1,2]{1,0:T(1,128)} %param.9) | copy-start | bytes 28
  5.6 44.0 %collective-permute-start.2 = (bf16[768,1280]{1,0:T(8,128)(2,1)}, bf16[768,1280]{1,0:T(8,128)(2,1)}, u32[]{:S(2)}, u32[]{:S(2)}) collective-permute-start(bf16[768,1280]{1,0:T(8,128)(2,1)} %slice.19), channel_id=1, source_target_pairs={{0,1},{1,0},{2,3},{3,2},{4,5},{5,4},{6,7},{7,6},{8,9},{9,8},{10,11... | collective-permute-start | bytes 5898248 | tf_op jit(solution)/shard_map/ppermute | solution.py:231
  7.0 42.5 %collective-permute-start.1 = (bf16[768,1280]{1,0:T(8,128)(2,1)}, bf16[768,1280]{1,0:T(8,128)(2,1)}, u32[]{:S(2)}, u32[]{:S(2)}) collective-permute-start(bf16[768,1280]{1,0:T(8,128)(2,1)} %slice.18), channel_id=1, source_target_pairs={{0,1},{1,0},{2,3},{3,2},{4,5},{5,4},{6,7},{7,6},{8,9},{9,8},{10,11... | collective-permute-start | bytes 5898248 | tf_op jit(solution)/shard_map/ppermute | solution.py:231
  8.4 8.2 %copy-start.4 = (s32[8]{0:T(128)S(1)}, s32[8]{0:T(128)}, u32[]{:S(2)}) copy-start(s32[8]{0:T(128)} %lengths.11) | copy-start | bytes 100
  8.4 8.2 %collective-permute-start.5 = (bf16[768,512]{1,0:T(8,128)(2,1)}, bf16[768,512]{1,0:T(8,128)(2,1)}, u32[]{:S(2)}, u32[]{:S(2)}) collective-permute-start(bf16[768,512]{1,0:T(8,128)(2,1)} %slice.22), channel_id=1, source_target_pairs={{0,1},{1,0},{2,3},{3,2},{4,5},{5,4},{6,7},{7,6},{8,9},{9,8},{10,11... | collective-permute-start | bytes 2359304 | tf_op jit(solution)/shard_map/ppermute | solution.py:231
  8.4 7.7 %collective-permute-start = (s32[1,2]{1,0:T(1,128)S(1)}, s32[1,2]{1,0:T(1,128)S(1)}, u32[]{:S(2)}, u32[]{:S(2)}) collective-permute-start(s32[1,2]{1,0:T(1,128)S(1)} %copy-done.5), channel_id=1, source_target_pairs={{0,8},{1,9},{2,10},{3,11},{4,12},{5,13},{6,14},{7,15},{8,0},{9,1},... | collective-permute-start | bytes 32 | tf_op jit(solution)/shard_map/ppermute | solution.py:220
  16.2 18.8 %collective-permute-start.4 = (bf16[768,768]{1,0:T(8,128)(2,1)}, bf16[768,768]{1,0:T(8,128)(2,1)S(1)}, u32[]{:S(2)}, u32[]{:S(2)}) collective-permute-start(bf16[768,768]{1,0:T(8,128)(2,1)} %slice.21), channel_id=1, source_target_pairs={{0,1},{1,0},{2,3},{3,2},{4,5},{5,4},{6,7},{7,6},{8,9},{9,8},{10,11... | collective-permute-start | bytes 3538952 | tf_op jit(solution)/shard_map/ppermute | solution.py:231
  16.2 18.8 %collective-permute-start.3 = (bf16[768,768]{1,0:T(8,128)(2,1)}, bf16[768,768]{1,0:T(8,128)(2,1)S(1)}, u32[]{:S(2)}, u32[]{:S(2)}) collective-permute-start(bf16[768,768]{1,0:T(8,128)(2,1)} %slice.20), channel_id=1, source_target_pairs={{0,1},{1,0},{2,3},{3,2},{4,5},{5,4},{6,7},{7,6},{8,9},{9,8},{10,11... | collective-permute-start | bytes 3538952 | tf_op jit(solution)/shard_map/ppermute | solution.py:231
  16.7 2.1 %copy-start.1 = (bf16[768,2560]{1,0:T(8,128)(2,1)S(1)}, bf16[768,2560]{1,0:T(8,128)(2,1)}, u32[]{:S(2)}) copy-start(bf16[768,2560]{1,0:T(8,128)(2,1)} %ko.11) | copy-start | bytes 11796484
  18.8 2.1 %copy-start.2 = (bf16[768,2560]{1,0:T(8,128)(2,1)S(1)}, bf16[768,2560]{1,0:T(8,128)(2,1)}, u32[]{:S(2)}) copy-start(bf16[768,2560]{1,0:T(8,128)(2,1)} %vo.11) | copy-start | bytes 11796484
  20.9 2.1 %copy-start.3 = (bf16[768,2560]{1,0:T(8,128)(2,1)S(1)}, bf16[768,2560]{1,0:T(8,128)(2,1)}, u32[]{:S(2)}) copy-start(bf16[768,2560]{1,0:T(8,128)(2,1)} %q.11) | copy-start | bytes 11796484
  27.1 47.2 %collective-permute-start.7 = (bf16[256,512]{1,0:T(8,128)(2,1)S(1)}, bf16[256,512]{1,0:T(8,128)(2,1)S(1)}, u32[]{:S(2)}, u32[]{:S(2)}) collective-permute-start(bf16[256,512]{1,0:T(8,128)(2,1)S(1)} %shard_map.71), channel_id=1, source_target_pairs={{0,8},{1,9},{2,10},{3,11},{4,12},{5,13},{6,14},{7,15},{8,0},{9,1},... | collective-permute-start | bytes 786440 | tf_op jit(solution)/shard_map/ppermute | solution.py:238
  39.6 34.7 %collective-permute-start.8 = (bf16[256,768]{1,0:T(8,128)(2,1)S(1)}, bf16[256,768]{1,0:T(8,128)(2,1)S(1)}, u32[]{:S(2)}, u32[]{:S(2)}) collective-permute-start(bf16[256,768]{1,0:T(8,128)(2,1)S(1)} %shard_map.72), channel_id=1, source_target_pairs={{0,8},{1,9},{2,10},{3,11},{4,12},{5,13},{6,14},{7,15},{8,0},{9,1},... | collective-permute-start | bytes 1179656 | tf_op jit(solution)/shard_map/ppermute | solution.py:238
  58.0 31.7 %collective-permute-start.9 = (bf16[256,1280]{1,0:T(8,128)(2,1)S(1)}, bf16[256,1280]{1,0:T(8,128)(2,1)S(1)}, u32[]{:S(2)}, u32[]{:S(2)}) collective-permute-start(bf16[256,1280]{1,0:T(8,128)(2,1)S(1)} %shard_map.73), channel_id=1, source_target_pairs={{0,8},{1,9},{2,10},{3,11},{4,12},{5,13},{6,14},{7,15},{8,0},{9,1},... | collective-permute-start | bytes 1966088 | tf_op jit(solution)/shard_map/ppermute | solution.py:238

commit v2 on v1

v2 whole, which is shorter than its diff:
```python
import math

import jax
import jax.numpy as jnp
from jax import lax
from jax.experimental import pallas as pl
from jax.experimental.pallas import tpu as pltpu
from jax.sharding import PartitionSpec as P

HD = 128
SLAB = 128
SPAN = 2
KEY_TILE = 256
KEY_CHUNK = 32
STEP_HEADS = 2
WIDTH = STEP_HEADS * HD
SCALE = math.log2(math.e) / math.sqrt(HD)
EARLY_HEADS = (4,)
LATER_HEADS = (6, 10)


def rows_of(start):
    return pl.ds(pl.multiple_of(start, SLAB), SLAB)


def scaled_queries(ref, slabs, columns):
    wide = jnp.concatenate([ref[rows_of(s * SLAB), columns] for s in slabs], axis=0)
    wide = wide.astype(jnp.float32) * SCALE
    high = wide.astype(jnp.bfloat16)
    low = (wide - high.astype(jnp.float32)).astype(jnp.bfloat16)
    return jnp.concatenate([high, low], axis=1)


def attend(q, tiles, slabs, scratch, store, opening=False, closing=False):
    scores, weights, peaks, totals = scratch
    rows = SLAB * len(slabs)
    for t in range(STEP_HEADS):
        columns = pl.ds(t * HD, HD)
        before = (t - 1) % STEP_HEADS
        if not closing:
            scaled = scaled_queries(q, slabs, columns)
        if not opening:
            value_rows = [ref[pl.ds(start, KEY_TILE), columns] for _, ref, start, _ in tiles]
            mixed = lax.dot_general(
                jnp.concatenate(value_rows, axis=0),
                weights[t][...],
                (((0,), (0,)), ((), ())),
                preferred_element_type=jnp.float32,
            )
            mixed = mixed / totals[t][0:1, :]
        weigh = (t > 0 or not opening) and (t == 0 or not closing)
        peak = jnp.full((8, rows), -jnp.inf, jnp.float32)
        total = jnp.zeros((8, rows), jnp.float32)
        old_peak = peaks[(t - 1) % 2][0:1, :]
        for j, (key_ref, _, start, limit) in enumerate(tiles):
            if not closing:
                keys = key_ref[pl.ds(start, KEY_TILE), columns]
                made = lax.dot_general(
                    jnp.concatenate([keys, keys], axis=1),
                    scaled,
                    (((1,), (1,)), ((), ())),
                    preferred_element_type=jnp.float32,
                )
                if limit is not None:
                    valid = lax.broadcasted_iota(jnp.int32, made.shape, 0) + start < limit
                    made = jnp.where(valid, made, -jnp.inf)
                scores[t % 2][pl.ds(j * KEY_TILE, KEY_TILE), :] = made
                peak = jnp.maximum(peak, jnp.max(made.reshape(KEY_TILE // 8, 8, rows), axis=0))
            for c in range(0, KEY_TILE if weigh else 0, KEY_CHUNK):
                here = pl.ds(j * KEY_TILE + c, KEY_CHUNK)
                weight = jnp.exp2(scores[(t - 1) % 2][here, :] - old_peak)
                total = total + jnp.sum(weight.reshape(KEY_CHUNK // 8, 8, rows), axis=0)
                weights[before][here, :] = weight.astype(jnp.bfloat16)
        if not closing:
            peaks[t % 2][...] = jnp.broadcast_to(jnp.max(peak, axis=0, keepdims=True), peak.shape)
        if weigh:
            totals[before][...] = jnp.broadcast_to(
                jnp.sum(total, axis=0, keepdims=True), total.shape
            )
        if not opening:
            store(t, slabs, mixed.T)


def attend_steps(active, *operands):
    step, last = pl.program_id(0), pl.num_programs(0) - 1

    @pl.when(active & (step == 0))
    def _():
        attend(*operands, opening=True)

    @pl.when(active & (step > 0) & (step < last))
    def _():
        attend(*operands)

    @pl.when(active & (step == last))
    def _():
        attend(*operands, closing=True)


def long_tiles(ko, vo, kx, vx, length, place):
    row_count = ko.shape[0]
    tiles = []
    for key_ref, value_ref, at in ((ko, vo, place), (kx, vx, 1 - place)):
        limit = jnp.clip(length - at * row_count, 0, row_count)
        for start in range(0, row_count, KEY_TILE):
            last = start + KEY_TILE == row_count
            tiles.append((key_ref, value_ref, start, limit if last else None))
    return tiles


def valid_part(result, n, slab, place, row_count, length):
    at = place * row_count + slab * SLAB + lax.broadcasted_iota(jnp.int32, (SLAB, HD), 0)
    return jnp.where(at < length, result[n * SLAB : (n + 1) * SLAB], 0.0).astype(jnp.bfloat16)


def help_body(me, lengths, listed, q, ko, vo, kx, vx, out, *scratch):
    row_count = q.shape[0]
    length = lengths[me[0] // SPAN]
    place = me[0] % SPAN
    active = listed[0, 0] >= 0
    slabs = [jnp.maximum(listed[0, n], 0) for n in range(listed.shape[1])]

    def store(h, slabs, result):
        for n, slab in enumerate(slabs):
            part = valid_part(result, n, slab, place, row_count, length)
            out[pl.ds(n * SLAB, SLAB), pl.ds(h * HD, HD)] = part

    tiles = long_tiles(ko, vo, kx, vx, length, place)
    attend_steps(active, q, tiles, slabs, grouped(scratch), store)

    @pl.when(jnp.logical_not(active))
    def _():
        out[...] = jnp.zeros_like(out)


def home_body(me, lengths, listed, q, ko, vo, kx, vx, out, *scratch):
    row_count = q.shape[0]
    length = lengths[me[0] // SPAN]
    place = me[0] % SPAN
    long = length > row_count
    short = jnp.logical_not(long)
    low = jnp.clip(jnp.minimum(listed[0, 0], listed[0, 1]), 0, row_count // SLAB - 2)
    high = jnp.clip(jnp.maximum(listed[0, 0], listed[0, 1]), 1, row_count // SLAB - 1)

    def store(h, slabs, result):
        for n, slab in enumerate(slabs):
            part = valid_part(result, n, slab, place, row_count, length)
            out[rows_of(slab * SLAB), pl.ds(h * HD, HD)] = part

    kept = []
    for n in range(row_count // SLAB - 2):
        slab = n + (n >= low).astype(jnp.int32)
        kept.append(slab + (slab >= high).astype(jnp.int32))
    tiles = long_tiles(ko, vo, kx, vx, length, place)
    attend_steps(long, q, tiles, kept, grouped(scratch[: len(scratch) // 2]), store)

    @pl.when(long)
    def _():
        for slab in (low, high):
            out[rows_of(slab * SLAB), :] = jnp.zeros((SLAB, WIDTH), jnp.bfloat16)

    tiles = [(ko, vo, start, length) for start in range(0, row_count, KEY_TILE)]
    slabs = list(range(row_count // SLAB))
    attend_steps(
        short & (place == 0), q, tiles, slabs, grouped(scratch[len(scratch) // 2 :]), store
    )

    @pl.when(short & (place == 1))
    def _():
        out[...] = jnp.zeros_like(out)


def scratch_of(keys, rows):
    scores = [pltpu.VMEM((keys, rows), jnp.float32)] * 2
    weights = [pltpu.VMEM((keys, rows), jnp.bfloat16)] * STEP_HEADS
    sides = [pltpu.VMEM((8, rows), jnp.float32)] * (2 + STEP_HEADS)
    return scores + weights + sides


def grouped(refs):
    edges = (0, 2, 2 + STEP_HEADS, 4 + STEP_HEADS, 4 + 2 * STEP_HEADS)
    return [refs[a:b] for a, b in zip(edges[:-1], edges[1:])]


def call(body, scalars, q, k, v, kx, vx, first, heads, rows, k_first, v_first):
    row_count, features = q.shape
    steps = heads // STEP_HEADS

    def block(height, at, lag):
        if lag:
            return pl.BlockSpec((height, WIDTH), lambda g, *_: (0, at + jnp.maximum(g - 1, 0)))
        return pl.BlockSpec((height, WIDTH), lambda g, *_: (0, at + jnp.minimum(g, steps - 1)))

    at = first // STEP_HEADS
    home = rows == row_count
    item = rows - 2 * SLAB if home else rows
    scratch = scratch_of(SPAN * row_count, item)
    if home:
        scratch += scratch_of(row_count, row_count)
    return pl.pallas_call(
        body,
        out_shape=jax.ShapeDtypeStruct((rows, heads * HD), jnp.bfloat16),
        grid_spec=pltpu.PrefetchScalarGridSpec(
            num_scalar_prefetch=len(scalars),
            grid=(steps + 1,),
            in_specs=[
                block(row_count, at, 0),
                block(row_count, at, 0),
                block(row_count, at, 1),
                block(row_count, k_first // STEP_HEADS, 0),
                block(row_count, v_first // STEP_HEADS, 1),
            ],
            out_specs=block(rows, 0, 1),
            scratch_shapes=scratch,
        ),
        compiler_params=pltpu.CompilerParams(
            vmem_limit_bytes=60 << 20, dimension_semantics=("arbitrary",)
        ),
        cost_estimate=pl.CostEstimate(
            flops=8 * item * SPAN * row_count * heads * HD,
            bytes_accessed=2 * 6 * row_count * heads * HD,
            transcendentals=item * SPAN * row_count * heads,
        ),
    )(*scalars, q, k, v, kx, vx)


def local(queries, keys, values, lengths, help_table):
    row_count, features = queries.shape
    size = lax.axis_size("seq")
    core_pairs = [(i, i ^ 1) for i in range(size)]
    far_pairs = [(i, i ^ size // 2) for i in range(size)]
    me = lax.axis_index("seq").astype(jnp.int32).reshape(1)
    listed_rows = help_table.shape[1] * SLAB

    sources = []
    first = 0
    packed = []
    for heads in EARLY_HEADS:
        columns = slice(first * HD, (first + heads) * HD)
        packed += [keys[:, columns], values[:, columns]]
        first += heads
    packed = lax.ppermute(packed, "seq", core_pairs)
    listed = lax.ppermute(help_table, "seq", far_pairs)
    first = 0
    for n, heads in enumerate(EARLY_HEADS):
        sources.append((packed[2 * n], packed[2 * n + 1], first, heads, 0, 0))
        first += heads
    keys_whole, values_whole, listed, *_ = lax.optimization_barrier(
        (keys, values, listed, *packed)
    )
    kx, vx = lax.ppermute((keys_whole, values_whole), "seq", core_pairs)
    for heads in LATER_HEADS:
        sources.append((kx, vx, first, heads, first, first))
        first += heads
    assert first * HD == features

    scalars = (me, lengths, listed)
    helped = []
    for kx_n, vx_n, first, heads, k_first, v_first in sources:
        outputs = call(
            help_body, scalars, queries, keys, values, kx_n, vx_n, first, heads, listed_rows,
            k_first, v_first,
        )
        helped.append(lax.ppermute(outputs, "seq", far_pairs))
    attended = call(
        home_body, scalars, queries, keys, values, kx, vx, 0, features // HD, row_count, 0, 0
    )
    return attended, jnp.concatenate(helped, axis=1)


def solution(mesh):
    rows = P(("groups", "seq"), None)
    return jax.shard_map(
        local,
        mesh=mesh,
        in_specs=(rows, rows, rows, P("groups"), rows),
        out_specs=(rows, rows),
        check_vma=False,
    )
```

time: 90.7 us -> 79.5 us (0.88)
  local copies, waits for them, and re-layouts: 16.6 us -> 2.93 us
  Pallas kernels: 51.1 us -> 49.2 us
  waiting for transfers between devices: 15.4 us -> 17.2 us
  starting transfers between devices: 5.95 us -> 7.66 us
    slice x6 -> x2, local copies, waits for them, and re-layouts: 10.3 us -> 2.37 us  [local(): packed += [keys[:, columns], values[:, columns]]]
    unnamed x12 -> x8, local copies, waits for them, and re-layouts: 6.35 us -> 0.55 us
    ppermute x6 -> x4, waiting for transfers between devices: 0.02 us -> 4.73 us  [the longest x2 4.72 us: local(): kx, vx = lax.ppermute((keys_whole, values_whole), 'seq', core_pairs)]
    ppermute x3, waiting for transfers between devices: 15.4 us -> 11 us  [local(): helped.append(lax.ppermute(outputs, 'seq', far_pairs))]
    ppermute x3, starting transfers between devices: 0.21 us -> 2.42 us  [local(): helped.append(lax.ppermute(outputs, 'seq', far_pairs))]
    pallas_call x6 -> x4, Pallas kernels: 51.1 us -> 49.2 us  [call(): pl.pallas_call(body, out_shape=jax.ShapeDtypeStruct((rows, heads * HD), j...]
    ppermute x1, waiting for transfers between devices: 0.01 us -> 1.52 us  [local(): listed = lax.ppermute(help_table, 'seq', far_pairs)]
  transfers between devices with their start and end apart: 10 -> 8, of which waited for: 1 -> 3; matrix products, arithmetic and copies ran while one was open for 10% -> 2% of each run, Pallas kernels for 56% -> 62%
where the time goes in v2:
time: 79.5 us; the launch traced here: 78.8 us
  Pallas kernels  49.2 us (62%)
  waiting for transfers between devices  17.2 us (22%)
  starting transfers between devices  7.66 us (10%)
  local copies, waits for them, and re-layouts  2.93 us (4%)
  other arithmetic  1.14 us (1%)
    pallas_call x4, Pallas kernels, call(): pl.pallas_call(body, out_shape=jax.ShapeDtypeStruct((rows, heads * HD), j...  49.2 us
    ppermute x3, waiting for transfers between devices, local(): helped.append(lax.ppermute(outputs, 'seq', far_pairs))  11 us
    ppermute x2, waiting for transfers between devices, local(): kx, vx = lax.ppermute((keys_whole, values_whole), 'seq', core_pairs)  4.72 us
    ppermute x1, starting transfers between devices, local(): listed = lax.ppermute(help_table, 'seq', far_pairs)  4.04 us
    ppermute x3, starting transfers between devices, local(): helped.append(lax.ppermute(outputs, 'seq', far_pairs))  2.42 us
    slice x2, local copies, waits for them, and re-layouts, local(): packed += [keys[:, columns], values[:, columns]]  2.37 us
  transfers between devices with their start and end apart: 8, of which 3 were waited for; matrix products, arithmetic and copies ran while one was open for 2% of the time, Pallas kernels for 62%

profile of v2, /device:TPU:0, one launch (start us, length us, event | category | flops | bytes accessed | tf_op | source)
XLA Modules:
  0.0 78.8 jit_solution(2122386338094994783)
XLA Ops:
  0.6 0.0 copy-start.3
  0.6 1.2 %slice.7 = bf16[768,512]{1,0:T(8,128)(2,1)S(1)} slice(bf16[768,2560]{1,0:T(8,128)(2,1)} %vo.7), slice={[0:768], [0:512]} | slice | bytes 1572864 | tf_op jit(solution)/shard_map/slice | solution.py:240
  1.8 0.5 collective-permute-start.2
  2.4 1.2 %slice.6 = bf16[768,512]{1,0:T(8,128)(2,1)S(1)} slice(bf16[768,2560]{1,0:T(8,128)(2,1)} %ko.7), slice={[0:768], [0:512]} | slice | bytes 1572864 | tf_op jit(solution)/shard_map/slice | solution.py:240
  3.5 0.1 collective-permute-start.1
  3.7 0.0 copy-done.3
  3.7 4.0 %collective-permute-start = (s32[1,2]{1,0:T(1,128)S(1)}, s32[1,2]{1,0:T(1,128)S(1)}, u32[]{:S(2)}, u32[]{:S(2)}) collective-permute-start(s32[1,2]{1,0:T(1,128)S(1)} %copy-done.3), channel_id=1, source_target_pairs={{0,8},{1,9},{2,10},{3,11},{4,12},{5,13},{6,14},{7,15},{8,0},{9,1},... | collective-permute-start | bytes 32 | tf_op jit(solution)/shard_map/ppermute | solution.py:243
  7.7 1.5 %collective-permute-done.listed = s32[1,2]{1,0:T(1,128)S(1)} collective-permute-done((s32[1,2]{1,0:T(1,128)S(1)}, s32[1,2]{1,0:T(1,128)S(1)}, u32[]{:S(2)}, u32[]{:S(2)}) %collective-permute-start) | collective-permute-done | bytes 40 | tf_op jit(solution)/shard_map/ppermute | solution.py:243
  9.2 0.0 copy-start.2
  9.2 0.0 collective-permute-done.2.vx
  9.2 0.0 copy-start
  9.2 0.0 collective-permute-done.1.kx
  9.2 0.0 copy-start.1
  9.2 0.1 collective-permute-start.3
  9.3 0.5 collective-permute-start.4
  9.8 0.0 copy-done.2
  9.8 0.3 copy-done
  10.1 0.3 copy-done.1
  10.4 5.4 %shard_map.69 = bf16[256,512]{1,0:T(8,128)(2,1)} custom-call(s32[1]{0:T(128)} %bitcast.me, s32[8]{0:T(128)} %lengths.7, s32[1,2]{1,0:T(1,128)} %copy-done.2, bf16[768,2560]{1,0:T(8,128)(2,1)} %q.7, bf16[768,2560]{1,0:T(8,128)(2,1)} %ko.7, bf16[768,2560]{1,0:T(8,128)(2,1)} %vo.7, bf16[768,512]{1,0:T(8,128)(2,1)} %copy-done.1, bf16[768,512]{1,0:T(8,128)(2,1)} %copy-done), custom_call_target="tpu_custom_call" | custom-call | flops 1610612736 | bytes 4718592 | tf_op jit(solution)/shard_map/pallas_call | solution.py:200
  15.7 1.6 %collective-permute-start.5 = (bf16[256,512]{1,0:T(8,128)(2,1)}, bf16[256,512]{1,0:T(8,128)(2,1)S(1)}, u32[]{:S(2)}, u32[]{:S(2)}) collective-permute-start(bf16[256,512]{1,0:T(8,128)(2,1)} %shard_map.69), channel_id=1, source_target_pairs={{0,8},{1,9},{2,10},{3,11},{4,12},{5,13},{6,14},{7,15},{8,0},{9,1},... | collective-permute-start | bytes 786440 | tf_op jit(solution)/shard_map/ppermute | solution.py:264
  17.3 0.0 collective-permute-done.3.kx
  17.3 4.7 %collective-permute-done.4.vx = bf16[768,2560]{1,0:T(8,128)(2,1)} collective-permute-done((bf16[768,2560]{1,0:T(8,128)(2,1)}, bf16[768,2560]{1,0:T(8,128)(2,1)}, u32[]{:S(2)}, u32[]{:S(2)}) %collective-permute-start.4) | collective-permute-done | bytes 3932192 | tf_op jit(solution)/shard_map/ppermute | solution.py:251
  22.1 6.9 %shard_map.70 = bf16[256,768]{1,0:T(8,128)(2,1)} custom-call(s32[1]{0:T(128)} %bitcast.me, s32[8]{0:T(128)} %lengths.7, s32[1,2]{1,0:T(1,128)} %copy-done.2, bf16[768,2560]{1,0:T(8,128)(2,1)} %q.7, bf16[768,2560]{1,0:T(8,128)(2,1)} %ko.7, bf16[768,2560]{1,0:T(8,128)(2,1)} %vo.7, bf16[768,2560]{1,0:T(8,128)(2,1)} %collective-permute-done.3.kx, ...), custom_call_target="tpu_custom_call" | custom-call | flops 2415919104 | bytes 7077888 | tf_op jit(solution)/shard_map/pallas_call | solution.py:200
  28.9 0.8 %collective-permute-start.6 = (bf16[256,768]{1,0:T(8,128)(2,1)}, bf16[256,768]{1,0:T(8,128)(2,1)S(1)}, u32[]{:S(2)}, u32[]{:S(2)}) collective-permute-start(bf16[256,768]{1,0:T(8,128)(2,1)} %shard_map.70), channel_id=1, source_target_pairs={{0,8},{1,9},{2,10},{3,11},{4,12},{5,13},{6,14},{7,15},{8,0},{9,1},... | collective-permute-start | bytes 1179656 | tf_op jit(solution)/shard_map/ppermute | solution.py:264
  29.7 9.5 %shard_map.71 = bf16[256,1280]{1,0:T(8,128)(2,1)} custom-call(s32[1]{0:T(128)} %bitcast.me, s32[8]{0:T(128)} %lengths.7, s32[1,2]{1,0:T(1,128)} %copy-done.2, bf16[768,2560]{1,0:T(8,128)(2,1)} %q.7, bf16[768,2560]{1,0:T(8,128)(2,1)} %ko.7, bf16[768,2560]{1,0:T(8,128)(2,1)} %vo.7, bf16[768,2560]{1,0:T(8,128)(2,1)} %collective-permute-done.3.kx, ...), custom_call_target="tpu_custom_call" | custom-call | flops 4026531840 | bytes 11796480 | tf_op jit(solution)/shard_map/pallas_call | solution.py:200
  39.2 0.0 collective-permute-start.7
  39.2 27.5 %shard_map.68 = bf16[768,2560]{1,0:T(8,128)(2,1)} custom-call(s32[1]{0:T(128)} %bitcast.me, s32[8]{0:T(128)} %lengths.7, s32[1,2]{1,0:T(1,128)} %copy-done.2, bf16[768,2560]{1,0:T(8,128)(2,1)} %q.7, bf16[768,2560]{1,0:T(8,128)(2,1)} %ko.7, bf16[768,2560]{1,0:T(8,128)(2,1)} %vo.7, bf16[768,2560]{1,0:T(8,128)(2,1)} %collective-permute-done.3.kx, ...), custom_call_target="tpu_custom_call" | custom-call | flops 16106127360 | bytes 23592960 | tf_op jit(solution)/shard_map/pallas_call | solution.py:200
  66.7 0.0 collective-permute-done.5
  66.7 0.0 collective-permute-done.6
  66.7 11.0 %collective-permute-done.7 = bf16[256,1280]{1,0:T(8,128)(2,1)S(1)} collective-permute-done((bf16[256,1280]{1,0:T(8,128)(2,1)}, bf16[256,1280]{1,0:T(8,128)(2,1)S(1)}, u32[]{:S(2)}, u32[]{:S(2)}) %collective-permute-start.7) | collective-permute-done | bytes 655392 | tf_op jit(solution)/shard_map/ppermute | solution.py:264
  77.7 1.1 %pad_maximum_fusion = bf16[256,2560]{1,0:T(8,128)(2,1)} fusion(bf16[256,1280]{1,0:T(8,128)(2,1)S(1)} %collective-permute-done.7, bf16[256,768]{1,0:T(8,128)(2,1)S(1)} %collective-permute-done.6, bf16[256,512]{1,0:T(8,128)(2,1)S(1)} %collective-permute-done.5), kind=kLoop, calls=%fused_computation | loop fusion | flops 3932160 | bytes 2621440 | tf_op jit(solution)/shard_map/concatenate | solution.py:268
Async XLA Ops:
  0.6 3.0 %copy-start.3 = (s32[1,2]{1,0:T(1,128)S(1)}, s32[1,2]{1,0:T(1,128)}, u32[]{:S(2)}) copy-start(s32[1,2]{1,0:T(1,128)} %param.9) | copy-start | bytes 28
  1.8 7.4 %collective-permute-start.2 = (bf16[768,512]{1,0:T(8,128)(2,1)S(1)}, bf16[768,512]{1,0:T(8,128)(2,1)S(1)}, u32[]{:S(2)}, u32[]{:S(2)}) collective-permute-start(bf16[768,512]{1,0:T(8,128)(2,1)S(1)} %slice.7), channel_id=1, source_target_pairs={{0,1},{1,0},{2,3},{3,2},{4,5},{5,4},{6,7},{7,6},{8,9},{9,8},{10,11... | collective-permute-start | bytes 2359304 | tf_op jit(solution)/shard_map/ppermute | solution.py:242
  3.5 5.7 %collective-permute-start.1 = (bf16[768,512]{1,0:T(8,128)(2,1)S(1)}, bf16[768,512]{1,0:T(8,128)(2,1)S(1)}, u32[]{:S(2)}, u32[]{:S(2)}) collective-permute-start(bf16[768,512]{1,0:T(8,128)(2,1)S(1)} %slice.6), channel_id=1, source_target_pairs={{0,1},{1,0},{2,3},{3,2},{4,5},{5,4},{6,7},{7,6},{8,9},{9,8},{10,11... | collective-permute-start | bytes 2359304 | tf_op jit(solution)/shard_map/ppermute | solution.py:242
  3.7 5.6 %collective-permute-start = (s32[1,2]{1,0:T(1,128)S(1)}, s32[1,2]{1,0:T(1,128)S(1)}, u32[]{:S(2)}, u32[]{:S(2)}) collective-permute-start(s32[1,2]{1,0:T(1,128)S(1)} %copy-done.3), channel_id=1, source_target_pairs={{0,8},{1,9},{2,10},{3,11},{4,12},{5,13},{6,14},{7,15},{8,0},{9,1},... | collective-permute-start | bytes 32 | tf_op jit(solution)/shard_map/ppermute | solution.py:243
  9.2 0.6 copy-start.2
  9.2 0.9 %copy-start = (bf16[768,512]{1,0:T(8,128)(2,1)}, bf16[768,512]{1,0:T(8,128)(2,1)S(1)}, u32[]{:S(2)}) copy-start(bf16[768,512]{1,0:T(8,128)(2,1)S(1)} %collective-permute-done.2.vx) | copy-start | bytes 2359300
  9.2 1.1 %copy-start.1 = (bf16[768,512]{1,0:T(8,128)(2,1)}, bf16[768,512]{1,0:T(8,128)(2,1)S(1)}, u32[]{:S(2)}) copy-start(bf16[768,512]{1,0:T(8,128)(2,1)S(1)} %collective-permute-done.1.kx) | copy-start | bytes 2359300
  9.2 8.1 %collective-permute-start.3 = (bf16[768,2560]{1,0:T(8,128)(2,1)}, bf16[768,2560]{1,0:T(8,128)(2,1)}, u32[]{:S(2)}, u32[]{:S(2)}) collective-permute-start(bf16[768,2560]{1,0:T(8,128)(2,1)} %ko.7), channel_id=1, source_target_pairs={{0,1},{1,0},{2,3},{3,2},{4,5},{5,4},{6,7},{7,6},{8,9},{9,8},{10,11... | collective-permute-start | bytes 11796488 | tf_op jit(solution)/shard_map/ppermute | solution.py:251
  9.3 12.7 %collective-permute-start.4 = (bf16[768,2560]{1,0:T(8,128)(2,1)}, bf16[768,2560]{1,0:T(8,128)(2,1)}, u32[]{:S(2)}, u32[]{:S(2)}) collective-permute-start(bf16[768,2560]{1,0:T(8,128)(2,1)} %vo.7), channel_id=1, source_target_pairs={{0,1},{1,0},{2,3},{3,2},{4,5},{5,4},{6,7},{7,6},{8,9},{9,8},{10,11... | collective-permute-start | bytes 11796488 | tf_op jit(solution)/shard_map/ppermute | solution.py:251
  15.7 51.0 %collective-permute-start.5 = (bf16[256,512]{1,0:T(8,128)(2,1)}, bf16[256,512]{1,0:T(8,128)(2,1)S(1)}, u32[]{:S(2)}, u32[]{:S(2)}) collective-permute-start(bf16[256,512]{1,0:T(8,128)(2,1)} %shard_map.69), channel_id=1, source_target_pairs={{0,8},{1,9},{2,10},{3,11},{4,12},{5,13},{6,14},{7,15},{8,0},{9,1},... | collective-permute-start | bytes 786440 | tf_op jit(solution)/shard_map/ppermute | solution.py:264
  28.9 37.8 %collective-permute-start.6 = (bf16[256,768]{1,0:T(8,128)(2,1)}, bf16[256,768]{1,0:T(8,128)(2,1)S(1)}, u32[]{:S(2)}, u32[]{:S(2)}) collective-permute-start(bf16[256,768]{1,0:T(8,128)(2,1)} %shard_map.70), channel_id=1, source_target_pairs={{0,8},{1,9},{2,10},{3,11},{4,12},{5,13},{6,14},{7,15},{8,0},{9,1},... | collective-permute-start | bytes 1179656 | tf_op jit(solution)/shard_map/ppermute | solution.py:264
  39.2 38.5 %collective-permute-start.7 = (bf16[256,1280]{1,0:T(8,128)(2,1)}, bf16[256,1280]{1,0:T(8,128)(2,1)S(1)}, u32[]{:S(2)}, u32[]{:S(2)}) collective-permute-start(bf16[256,1280]{1,0:T(8,128)(2,1)} %shard_map.71), channel_id=1, source_target_pairs={{0,8},{1,9},{2,10},{3,11},{4,12},{5,13},{6,14},{7,15},{8,0},{9,1},... | collective-permute-start | bytes 1966088 | tf_op jit(solution)/shard_map/ppermute | solution.py:264

commit v3 on v2

--- a/solution.py
+++ b/solution.py
@@ -15,8 +15,10 @@
 STEP_HEADS = 2
 WIDTH = STEP_HEADS * HD
 SCALE = math.log2(math.e) / math.sqrt(HD)
-EARLY_HEADS = (4,)
-LATER_HEADS = (6, 10)
+EARLY_HEADS = (2, 4)
+LATER_HEADS = (6, 8)
+HELP_VMEM = 16 << 20
+HOME_VMEM = 26 << 20
 
 
 def rows_of(start):
@@ -182,8 +184,8 @@
     return [refs[a:b] for a, b in zip(edges[:-1], edges[1:])]
 
 
-def call(body, scalars, q, k, v, kx, vx, first, heads, rows, k_first, v_first):
-    row_count, features = q.shape
+def call(body, scalars, arrays, first, heads, rows, vmem):
+    row_count = arrays[0].shape[0]
     steps = heads // STEP_HEADS
 
     def block(height, at, lag):
@@ -207,21 +209,21 @@
                 block(row_count, at, 0),
                 block(row_count, at, 0),
                 block(row_count, at, 1),
-                block(row_count, k_first // STEP_HEADS, 0),
-                block(row_count, v_first // STEP_HEADS, 1),
+                block(row_count, at, 0),
+                block(row_count, at, 1),
             ],
             out_specs=block(rows, 0, 1),
             scratch_shapes=scratch,
         ),
         compiler_params=pltpu.CompilerParams(
-            vmem_limit_bytes=60 << 20, dimension_semantics=("arbitrary",)
+            vmem_limit_bytes=vmem, dimension_semantics=("arbitrary",)
         ),
         cost_estimate=pl.CostEstimate(
             flops=8 * item * SPAN * row_count * heads * HD,
             bytes_accessed=2 * 6 * row_count * heads * HD,
             transcendentals=item * SPAN * row_count * heads,
         ),
-    )(*scalars, q, k, v, kx, vx)
+    )(*scalars, *arrays)
 
 
 def local(queries, keys, values, lengths, help_table):
@@ -232,39 +234,27 @@
     me = lax.axis_index("seq").astype(jnp.int32).reshape(1)
     listed_rows = help_table.shape[1] * SLAB
 
-    sources = []
-    first = 0
-    packed = []
-    for heads in EARLY_HEADS:
-        columns = slice(first * HD, (first + heads) * HD)
-        packed += [keys[:, columns], values[:, columns]]
-        first += heads
-    packed = lax.ppermute(packed, "seq", core_pairs)
+    early = sum(EARLY_HEADS) * HD
+    q_early, k_early, v_early = (x[:, :early] for x in (queries, keys, values))
+    kx_early, vx_early = lax.ppermute((k_early, v_early), "seq", core_pairs)
     listed = lax.ppermute(help_table, "seq", far_pairs)
-    first = 0
-    for n, heads in enumerate(EARLY_HEADS):
-        sources.append((packed[2 * n], packed[2 * n + 1], first, heads, 0, 0))
-        first += heads
-    keys_whole, values_whole, listed, *_ = lax.optimization_barrier(
-        (keys, values, listed, *packed)
+    keys_whole, values_whole, listed, _, _ = lax.optimization_barrier(
+        (keys, values, listed, kx_early, vx_early)
     )
     kx, vx = lax.ppermute((keys_whole, values_whole), "seq", core_pairs)
-    for heads in LATER_HEADS:
-        sources.append((kx, vx, first, heads, first, first))
+    scalars = (me, lengths, listed)
+    early_arrays = (q_early, k_early, v_early, kx_early, vx_early)
+    arrays = (queries, keys, values, kx, vx)
+
+    helped = []
+    first = 0
+    for n, heads in enumerate(EARLY_HEADS + LATER_HEADS):
+        sources = early_arrays if n < len(EARLY_HEADS) else arrays
+        outputs = call(help_body, scalars, sources, first, heads, listed_rows, HELP_VMEM)
+        helped.append(lax.ppermute(outputs, "seq", far_pairs))
         first += heads
     assert first * HD == features
-
-    scalars = (me, lengths, listed)
-    helped = []
-    for kx_n, vx_n, first, heads, k_first, v_first in sources:
-        outputs = call(
-            help_body, scalars, queries, keys, values, kx_n, vx_n, first, heads, listed_rows,
-            k_first, v_first,
-        )
-        helped.append(lax.ppermute(outputs, "seq", far_pairs))
-    attended = call(
-        home_body, scalars, queries, keys, values, kx, vx, 0, features // HD, row_count, 0, 0
-    )
+    attended = call(home_body, scalars, arrays, 0, first, row_count, HOME_VMEM)
     return attended, jnp.concatenate(helped, axis=1)
 
 

time: 79.5 us -> 76.4 us (0.961)
  Pallas kernels: 49.2 us -> 46.3 us
  waiting for transfers between devices: 17.2 us -> 14.4 us
  local copies, waits for them, and re-layouts: 2.93 us -> 5.35 us
    pallas_call x4 -> x5, Pallas kernels: 49.2 us -> 46.3 us  [call(): pl.pallas_call(body, out_shape=jax.ShapeDtypeStruct((rows, heads * HD), j...]
    slice x2 -> x3, local copies, waits for them, and re-layouts: 2.37 us -> 4.14 us  [local(): q_early, k_early, v_early = (x[:, :early] for x in (queries, keys, values))]
    ppermute x2, waiting for transfers between devices: 4.72 us -> 3.18 us  [local(): kx, vx = lax.ppermute((keys_whole, values_whole), 'seq', core_pairs)]
    ppermute x3 -> x4, waiting for transfers between devices: 11 us -> 9.7 us  [local(): helped.append(lax.ppermute(outputs, 'seq', far_pairs))]
    ppermute x3 -> x4, starting transfers between devices: 2.42 us -> 2.62 us  [local(): helped.append(lax.ppermute(outputs, 'seq', far_pairs))]
  transfers between devices with their start and end apart: 8 -> 9, of which waited for: 3 -> 3; matrix products, arithmetic and copies ran while one was open for 2% -> 4% of each run, Pallas kernels for 62% -> 61%
where the time goes in v3:
time: 76.4 us; the launch traced here: 75.8 us
  Pallas kernels  46.3 us (61%)
  waiting for transfers between devices  14.4 us (19%)
  starting transfers between devices  7.81 us (10%)
  local copies, waits for them, and re-layouts  5.35 us (7%)
  other arithmetic  1.14 us (1%)
    pallas_call x5, Pallas kernels, call(): pl.pallas_call(body, out_shape=jax.ShapeDtypeStruct((rows, heads * HD), j...  46.3 us
    ppermute x4, waiting for transfers between devices, local(): helped.append(lax.ppermute(outputs, 'seq', far_pairs))  9.7 us
    slice x3, local copies, waits for them, and re-layouts, local(): q_early, k_early, v_early = (x[:, :early] for x in (queries, keys, values))  4.14 us
    ppermute x1, starting transfers between devices, local(): listed = lax.ppermute(help_table, 'seq', far_pairs)  4.04 us
    ppermute x2, waiting for transfers between devices, local(): kx, vx = lax.ppermute((keys_whole, values_whole), 'seq', core_pairs)  3.18 us
    ppermute x4, starting transfers between devices, local(): helped.append(lax.ppermute(outputs, 'seq', far_pairs))  2.62 us
  transfers between devices with their start and end apart: 9, of which 3 were waited for; matrix products, arithmetic and copies ran while one was open for 4% of the time, Pallas kernels for 61%

profile of v3, /device:TPU:0, one launch (start us, length us, event | category | flops | bytes accessed | tf_op | source)
XLA Modules:
  0.0 75.8 jit_solution(10438785225419427757)
XLA Ops:
  0.6 0.0 copy-start.4
  0.6 1.4 %slice.10.vo = bf16[768,768]{1,0:T(8,128)(2,1)S(1)} slice(bf16[768,2560]{1,0:T(8,128)(2,1)} %vo.5), slice={[0:768], [0:768]} | slice | bytes 2359296 | tf_op jit(solution)/shard_map/slice | solution.py:238
  2.0 0.0 copy-start.3
  2.0 0.5 collective-permute-start.2
  2.5 1.3 %slice.9.ko = bf16[768,768]{1,0:T(8,128)(2,1)S(1)} slice(bf16[768,2560]{1,0:T(8,128)(2,1)} %ko.5), slice={[0:768], [0:768]} | slice | bytes 2359296 | tf_op jit(solution)/shard_map/slice | solution.py:238
  3.9 0.1 collective-permute-start.1
  4.0 0.0 copy-done.4
  4.0 4.0 %collective-permute-start = (s32[1,2]{1,0:T(1,128)S(1)}, s32[1,2]{1,0:T(1,128)S(1)}, u32[]{:S(2)}, u32[]{:S(2)}) collective-permute-start(s32[1,2]{1,0:T(1,128)S(1)} %copy-done.4), channel_id=1, source_target_pairs={{0,8},{1,9},{2,10},{3,11},{4,12},{5,13},{6,14},{7,15},{8,0},{9,1},... | collective-permute-start | bytes 32 | tf_op jit(solution)/shard_map/ppermute | solution.py:240
  8.0 1.5 %collective-permute-done.listed = s32[1,2]{1,0:T(1,128)S(1)} collective-permute-done((s32[1,2]{1,0:T(1,128)S(1)}, s32[1,2]{1,0:T(1,128)S(1)}, u32[]{:S(2)}, u32[]{:S(2)}) %collective-permute-start) | collective-permute-done | bytes 40 | tf_op jit(solution)/shard_map/ppermute | solution.py:240
  9.6 0.0 collective-permute-done.2.vx
  9.6 0.0 collective-permute-done.1.kx
  9.6 0.0 copy-start.1
  9.6 1.0 %copy-done.1 = bf16[768,768]{1,0:T(8,128)(2,1)} copy-done((bf16[768,768]{1,0:T(8,128)(2,1)}, bf16[768,768]{1,0:T(8,128)(2,1)S(1)}, u32[]{:S(2)}) %copy-start.1) | copy-done | bytes 1179672
  10.6 0.0 collective-permute-start.3
  10.6 0.5 collective-permute-start.4
  11.1 0.0 copy-start.2
  11.1 1.4 %slice.11.q = bf16[768,768]{1,0:T(8,128)(2,1)S(1)} slice(bf16[768,2560]{1,0:T(8,128)(2,1)} %q.5), slice={[0:768], [0:768]} | slice | bytes 2359296 | tf_op jit(solution)/shard_map/slice | solution.py:238
  12.5 0.0 copy-done.3
  12.5 0.2 copy-done.2
  12.7 2.1 %shard_map.69 = bf16[256,256]{1,0:T(8,128)(2,1)S(1)} custom-call(s32[1]{0:T(128)} %bitcast.me, s32[8]{0:T(128)S(1)} %copy-done.3, s32[1,2]{1,0:T(1,128)S(1)} %collective-permute-done.listed, bf16[768,768]{1,0:T(8,128)(2,1)S(1)} %slice.11.q, bf16[768,768]{1,0:T(8,128)(2,1)S(1)} %slice.9.ko, bf16[768,768]{1,0:T(8,128)(2,1)S(1)} %slice.10.vo, ...), custom_call_target="tpu_custom_call" | custom-call | flops 805306368 | bytes 2359296 | tf_op jit(solution)/shard_map/pallas_call | solution.py:202
  14.9 0.0 copy-start
  14.9 1.7 %collective-permute-start.5 = (bf16[256,256]{1,0:T(8,128)(2,1)S(1)}, bf16[256,256]{1,0:T(8,128)(2,1)S(1)}, u32[]{:S(2)}, u32[]{:S(2)}) collective-permute-start(bf16[256,256]{1,0:T(8,128)(2,1)S(1)} %shard_map.69), channel_id=1, source_target_pairs={{0,8},{1,9},{2,10},{3,11},{4,12},{5,13},{6,14},{7,15},{8,0},{9,1},... | collective-permute-start | bytes 393224 | tf_op jit(solution)/shard_map/ppermute | solution.py:254
  16.6 3.5 %shard_map.70 = bf16[256,512]{1,0:T(8,128)(2,1)S(1)} custom-call(s32[1]{0:T(128)} %bitcast.me, s32[8]{0:T(128)S(1)} %copy-done.3, s32[1,2]{1,0:T(1,128)S(1)} %collective-permute-done.listed, bf16[768,768]{1,0:T(8,128)(2,1)S(1)} %slice.11.q, bf16[768,768]{1,0:T(8,128)(2,1)S(1)} %slice.9.ko, bf16[768,768]{1,0:T(8,128)(2,1)S(1)} %slice.10.vo, ...), custom_call_target="tpu_custom_call" | custom-call | flops 1610612736 | bytes 4718592 | tf_op jit(solution)/shard_map/pallas_call | solution.py:202
  20.1 0.1 collective-permute-start.6
  20.1 0.0 collective-permute-done.3.kx
  20.1 3.2 %collective-permute-done.4.vx = bf16[768,2560]{1,0:T(8,128)(2,1)} collective-permute-done((bf16[768,2560]{1,0:T(8,128)(2,1)}, bf16[768,2560]{1,0:T(8,128)(2,1)}, u32[]{:S(2)}, u32[]{:S(2)}) %collective-permute-start.4) | collective-permute-done | bytes 3932192 | tf_op jit(solution)/shard_map/ppermute | solution.py:244
  23.3 0.0 copy-done
  23.3 5.9 %shard_map.71 = bf16[256,768]{1,0:T(8,128)(2,1)S(1)} custom-call(s32[1]{0:T(128)} %bitcast.me, s32[8]{0:T(128)S(1)} %copy-done.3, s32[1,2]{1,0:T(1,128)S(1)} %collective-permute-done.listed, bf16[768,2560]{1,0:T(8,128)(2,1)S(1)} %copy-done, bf16[768,2560]{1,0:T(8,128)(2,1)} %ko.5, bf16[768,2560]{1,0:T(8,128)(2,1)} %vo.5, ...), custom_call_target="tpu_custom_call" | custom-call | flops 2415919104 | bytes 7077888 | tf_op jit(solution)/shard_map/pallas_call | solution.py:202
  29.3 0.8 %collective-permute-start.7 = (bf16[256,768]{1,0:T(8,128)(2,1)S(1)}, bf16[256,768]{1,0:T(8,128)(2,1)S(1)}, u32[]{:S(2)}, u32[]{:S(2)}) collective-permute-start(bf16[256,768]{1,0:T(8,128)(2,1)S(1)} %shard_map.71), channel_id=1, source_target_pairs={{0,8},{1,9},{2,10},{3,11},{4,12},{5,13},{6,14},{7,15},{8,0},{9,1},... | collective-permute-start | bytes 1179656 | tf_op jit(solution)/shard_map/ppermute | solution.py:254
  30.1 7.2 %shard_map.72 = bf16[256,1024]{1,0:T(8,128)(2,1)S(1)} custom-call(s32[1]{0:T(128)} %bitcast.me, s32[8]{0:T(128)S(1)} %copy-done.3, s32[1,2]{1,0:T(1,128)S(1)} %collective-permute-done.listed, bf16[768,2560]{1,0:T(8,128)(2,1)S(1)} %copy-done, bf16[768,2560]{1,0:T(8,128)(2,1)} %ko.5, bf16[768,2560]{1,0:T(8,128)(2,1)} %vo.5, ...), custom_call_target="tpu_custom_call" | custom-call | flops 3221225472 | bytes 9437184 | tf_op jit(solution)/shard_map/pallas_call | solution.py:202
  37.2 0.1 collective-permute-start.8
  37.3 27.6 %shard_map.68 = bf16[768,2560]{1,0:T(8,128)(2,1)} custom-call(s32[1]{0:T(128)} %bitcast.me, s32[8]{0:T(128)S(1)} %copy-done.3, s32[1,2]{1,0:T(1,128)S(1)} %collective-permute-done.listed, bf16[768,2560]{1,0:T(8,128)(2,1)S(1)} %copy-done, bf16[768,2560]{1,0:T(8,128)(2,1)} %ko.5, bf16[768,2560]{1,0:T(8,128)(2,1)} %vo.5, ...), custom_call_target="tpu_custom_call" | custom-call | flops 16106127360 | bytes 23592960 | tf_op jit(solution)/shard_map/pallas_call | solution.py:202
  64.9 0.0 collective-permute-done.5
  64.9 0.0 collective-permute-done.6
  64.9 0.0 collective-permute-done.7
  64.9 9.7 %collective-permute-done.8 = bf16[256,1024]{1,0:T(8,128)(2,1)S(1)} collective-permute-done((bf16[256,1024]{1,0:T(8,128)(2,1)S(1)}, bf16[256,1024]{1,0:T(8,128)(2,1)S(1)}, u32[]{:S(2)}, u32[]{:S(2)}) %collective-permute-start.8) | collective-permute-done | bytes 524320 | tf_op jit(solution)/shard_map/ppermute | solution.py:254
  74.6 1.1 %pad_maximum_fusion = bf16[256,2560]{1,0:T(8,128)(2,1)} fusion(bf16[256,1024]{1,0:T(8,128)(2,1)S(1)} %collective-permute-done.8, bf16[256,768]{1,0:T(8,128)(2,1)S(1)} %collective-permute-done.7, bf16[256,512]{1,0:T(8,128)(2,1)S(1)} %collective-permute-done.6, bf16[256,256]{1,0:T(8,128)(2,1)S(1)} %collective-permute-done.5), kind=kLoop, calls=%fused_computation | loop fusion | flops 5242880 | bytes 2621440 | tf_op jit(solution)/shard_map/concatenate | solution.py:258
Async XLA Ops:
  0.6 3.4 %copy-start.4 = (s32[1,2]{1,0:T(1,128)S(1)}, s32[1,2]{1,0:T(1,128)}, u32[]{:S(2)}) copy-start(s32[1,2]{1,0:T(1,128)} %param.9) | copy-start | bytes 28
  2.0 10.5 %copy-start.3 = (s32[8]{0:T(128)S(1)}, s32[8]{0:T(128)}, u32[]{:S(2)}) copy-start(s32[8]{0:T(128)} %lengths.9) | copy-start | bytes 100
  2.0 7.6 %collective-permute-start.2 = (bf16[768,768]{1,0:T(8,128)(2,1)S(1)}, bf16[768,768]{1,0:T(8,128)(2,1)S(1)}, u32[]{:S(2)}, u32[]{:S(2)}) collective-permute-start(bf16[768,768]{1,0:T(8,128)(2,1)S(1)} %slice.10.vo), channel_id=1, source_target_pairs={{0,1},{1,0},{2,3},{3,2},{4,5},{5,4},{6,7},{7,6},{8,9},{9,8},{10,11... | collective-permute-start | bytes 3538952 | tf_op jit(solution)/shard_map/ppermute | solution.py:239
  3.9 5.7 %collective-permute-start.1 = (bf16[768,768]{1,0:T(8,128)(2,1)S(1)}, bf16[768,768]{1,0:T(8,128)(2,1)S(1)}, u32[]{:S(2)}, u32[]{:S(2)}) collective-permute-start(bf16[768,768]{1,0:T(8,128)(2,1)S(1)} %slice.9.ko), channel_id=1, source_target_pairs={{0,1},{1,0},{2,3},{3,2},{4,5},{5,4},{6,7},{7,6},{8,9},{9,8},{10,11... | collective-permute-start | bytes 3538952 | tf_op jit(solution)/shard_map/ppermute | solution.py:239
  4.0 5.6 %collective-permute-start = (s32[1,2]{1,0:T(1,128)S(1)}, s32[1,2]{1,0:T(1,128)S(1)}, u32[]{:S(2)}, u32[]{:S(2)}) collective-permute-start(s32[1,2]{1,0:T(1,128)S(1)} %copy-done.4), channel_id=1, source_target_pairs={{0,8},{1,9},{2,10},{3,11},{4,12},{5,13},{6,14},{7,15},{8,0},{9,1},... | collective-permute-start | bytes 32 | tf_op jit(solution)/shard_map/ppermute | solution.py:240
  9.6 1.0 %copy-start.1 = (bf16[768,768]{1,0:T(8,128)(2,1)}, bf16[768,768]{1,0:T(8,128)(2,1)S(1)}, u32[]{:S(2)}) copy-start(bf16[768,768]{1,0:T(8,128)(2,1)S(1)} %collective-permute-done.1.kx) | copy-start | bytes 3538948
  10.6 9.6 %collective-permute-start.3 = (bf16[768,2560]{1,0:T(8,128)(2,1)}, bf16[768,2560]{1,0:T(8,128)(2,1)}, u32[]{:S(2)}, u32[]{:S(2)}) collective-permute-start(bf16[768,2560]{1,0:T(8,128)(2,1)} %ko.5), channel_id=1, source_target_pairs={{0,1},{1,0},{2,3},{3,2},{4,5},{5,4},{6,7},{7,6},{8,9},{9,8},{10,11... | collective-permute-start | bytes 11796488 | tf_op jit(solution)/shard_map/ppermute | solution.py:244
  10.6 12.7 %collective-permute-start.4 = (bf16[768,2560]{1,0:T(8,128)(2,1)}, bf16[768,2560]{1,0:T(8,128)(2,1)}, u32[]{:S(2)}, u32[]{:S(2)}) collective-permute-start(bf16[768,2560]{1,0:T(8,128)(2,1)} %vo.5), channel_id=1, source_target_pairs={{0,1},{1,0},{2,3},{3,2},{4,5},{5,4},{6,7},{7,6},{8,9},{9,8},{10,11... | collective-permute-start | bytes 11796488 | tf_op jit(solution)/shard_map/ppermute | solution.py:244
  11.1 1.6 %copy-start.2 = (bf16[768,768]{1,0:T(8,128)(2,1)S(1)}, bf16[768,768]{1,0:T(8,128)(2,1)}, u32[]{:S(2)}) copy-start(bf16[768,768]{1,0:T(8,128)(2,1)} %copy-done.1) | copy-start | bytes 3538948
  14.9 8.5 %copy-start = (bf16[768,2560]{1,0:T(8,128)(2,1)S(1)}, bf16[768,2560]{1,0:T(8,128)(2,1)}, u32[]{:S(2)}) copy-start(bf16[768,2560]{1,0:T(8,128)(2,1)} %q.5) | copy-start | bytes 11796484
  14.9 50.0 %collective-permute-start.5 = (bf16[256,256]{1,0:T(8,128)(2,1)S(1)}, bf16[256,256]{1,0:T(8,128)(2,1)S(1)}, u32[]{:S(2)}, u32[]{:S(2)}) collective-permute-start(bf16[256,256]{1,0:T(8,128)(2,1)S(1)} %shard_map.69), channel_id=1, source_target_pairs={{0,8},{1,9},{2,10},{3,11},{4,12},{5,13},{6,14},{7,15},{8,0},{9,1},... | collective-permute-start | bytes 393224 | tf_op jit(solution)/shard_map/ppermute | solution.py:254
  20.1 44.9 %collective-permute-start.6 = (bf16[256,512]{1,0:T(8,128)(2,1)S(1)}, bf16[256,512]{1,0:T(8,128)(2,1)S(1)}, u32[]{:S(2)}, u32[]{:S(2)}) collective-permute-start(bf16[256,512]{1,0:T(8,128)(2,1)S(1)} %shard_map.70), channel_id=1, source_target_pairs={{0,8},{1,9},{2,10},{3,11},{4,12},{5,13},{6,14},{7,15},{8,0},{9,1},... | collective-permute-start | bytes 786440 | tf_op jit(solution)/shard_map/ppermute | solution.py:254
  29.3 35.7 %collective-permute-start.7 = (bf16[256,768]{1,0:T(8,128)(2,1)S(1)}, bf16[256,768]{1,0:T(8,128)(2,1)S(1)}, u32[]{:S(2)}, u32[]{:S(2)}) collective-permute-start(bf16[256,768]{1,0:T(8,128)(2,1)S(1)} %shard_map.71), channel_id=1, source_target_pairs={{0,8},{1,9},{2,10},{3,11},{4,12},{5,13},{6,14},{7,15},{8,0},{9,1},... | collective-permute-start | bytes 1179656 | tf_op jit(solution)/shard_map/ppermute | solution.py:254
  37.2 37.4 %collective-permute-start.8 = (bf16[256,1024]{1,0:T(8,128)(2,1)S(1)}, bf16[256,1024]{1,0:T(8,128)(2,1)S(1)}, u32[]{:S(2)}, u32[]{:S(2)}) collective-permute-start(bf16[256,1024]{1,0:T(8,128)(2,1)S(1)} %shard_map.72), channel_id=1, source_target_pairs={{0,8},{1,9},{2,10},{3,11},{4,12},{5,13},{6,14},{7,15},{8,0},{9,1},... | collective-permute-start | bytes 1572872 | tf_op jit(solution)/shard_map/ppermute | solution.py:254

commit v4 on v3

--- a/solution.py
+++ b/solution.py
@@ -17,8 +17,8 @@
 SCALE = math.log2(math.e) / math.sqrt(HD)
 EARLY_HEADS = (2, 4)
 LATER_HEADS = (6, 8)
-HELP_VMEM = 16 << 20
-HOME_VMEM = 26 << 20
+HELP_VMEM = 12 << 20
+HOME_VMEM = 24 << 20
 
 
 def rows_of(start):
@@ -238,7 +238,7 @@
     q_early, k_early, v_early = (x[:, :early] for x in (queries, keys, values))
     kx_early, vx_early = lax.ppermute((k_early, v_early), "seq", core_pairs)
     listed = lax.ppermute(help_table, "seq", far_pairs)
-    keys_whole, values_whole, listed, _, _ = lax.optimization_barrier(
+    keys_whole, values_whole, listed, kx_early, vx_early = lax.optimization_barrier(
         (keys, values, listed, kx_early, vx_early)
     )
     kx, vx = lax.ppermute((keys_whole, values_whole), "seq", core_pairs)

time: 76.4 us -> 76.4 us (level)
  no operation moved by 1% of the time
where the time goes in v4:
time: 76.4 us; the launch traced here: 75.8 us
  Pallas kernels  46.3 us (61%)
  waiting for transfers between devices  14.4 us (19%)
  starting transfers between devices  7.81 us (10%)
  local copies, waits for them, and re-layouts  5.35 us (7%)
  other arithmetic  1.14 us (1%)
    pallas_call x5, Pallas kernels, call(): pl.pallas_call(body, out_shape=jax.ShapeDtypeStruct((rows, heads * HD), j...  46.3 us
    ppermute x4, waiting for transfers between devices, local(): helped.append(lax.ppermute(outputs, 'seq', far_pairs))  9.7 us
    slice x3, local copies, waits for them, and re-layouts, local(): q_early, k_early, v_early = (x[:, :early] for x in (queries, keys, values))  4.14 us
    ppermute x1, starting transfers between devices, local(): listed = lax.ppermute(help_table, 'seq', far_pairs)  4.04 us
    ppermute x2, waiting for transfers between devices, local(): kx, vx = lax.ppermute((keys_whole, values_whole), 'seq', core_pairs)  3.18 us
    ppermute x4, starting transfers between devices, local(): helped.append(lax.ppermute(outputs, 'seq', far_pairs))  2.62 us
  transfers between devices with their start and end apart: 9, of which 3 were waited for; matrix products, arithmetic and copies ran while one was open for 4% of the time, Pallas kernels for 61%

profile of v4, /device:TPU:0, one launch (start us, length us, event | category | flops | bytes accessed | tf_op | source)
XLA Modules:
  0.0 75.8 jit_solution(10491400772811317182)
XLA Ops:
  0.6 0.0 copy-start.4
  0.6 1.4 %slice.10.vo = bf16[768,768]{1,0:T(8,128)(2,1)S(1)} slice(bf16[768,2560]{1,0:T(8,128)(2,1)} %vo.5), slice={[0:768], [0:768]} | slice | bytes 2359296 | tf_op jit(solution)/shard_map/slice | solution.py:238
  2.0 0.0 copy-start.3
  2.0 0.5 collective-permute-start.2
  2.5 1.3 %slice.9.ko = bf16[768,768]{1,0:T(8,128)(2,1)S(1)} slice(bf16[768,2560]{1,0:T(8,128)(2,1)} %ko.5), slice={[0:768], [0:768]} | slice | bytes 2359296 | tf_op jit(solution)/shard_map/slice | solution.py:238
  3.9 0.1 collective-permute-start.1
  4.0 0.0 copy-done.4
  4.0 4.0 %collective-permute-start = (s32[1,2]{1,0:T(1,128)S(1)}, s32[1,2]{1,0:T(1,128)S(1)}, u32[]{:S(2)}, u32[]{:S(2)}) collective-permute-start(s32[1,2]{1,0:T(1,128)S(1)} %copy-done.4), channel_id=1, source_target_pairs={{0,8},{1,9},{2,10},{3,11},{4,12},{5,13},{6,14},{7,15},{8,0},{9,1},... | collective-permute-start | bytes 32 | tf_op jit(solution)/shard_map/ppermute | solution.py:240
  8.0 1.5 %collective-permute-done.listed = s32[1,2]{1,0:T(1,128)S(1)} collective-permute-done((s32[1,2]{1,0:T(1,128)S(1)}, s32[1,2]{1,0:T(1,128)S(1)}, u32[]{:S(2)}, u32[]{:S(2)}) %collective-permute-start) | collective-permute-done | bytes 40 | tf_op jit(solution)/shard_map/ppermute | solution.py:240
  9.6 0.0 collective-permute-done.2.vx
  9.6 0.0 collective-permute-done.1.kx
  9.6 0.0 copy-start.1
  9.6 1.0 %copy-done.1 = bf16[768,768]{1,0:T(8,128)(2,1)} copy-done((bf16[768,768]{1,0:T(8,128)(2,1)}, bf16[768,768]{1,0:T(8,128)(2,1)S(1)}, u32[]{:S(2)}) %copy-start.1) | copy-done | bytes 1179672
  10.6 0.0 collective-permute-start.3
  10.6 0.5 collective-permute-start.4
  11.1 0.0 copy-start.2
  11.1 1.4 %slice.11.q = bf16[768,768]{1,0:T(8,128)(2,1)S(1)} slice(bf16[768,2560]{1,0:T(8,128)(2,1)} %q.5), slice={[0:768], [0:768]} | slice | bytes 2359296 | tf_op jit(solution)/shard_map/slice | solution.py:238
  12.5 0.0 copy-done.3
  12.5 0.2 copy-done.2
  12.7 2.1 %shard_map.69 = bf16[256,256]{1,0:T(8,128)(2,1)S(1)} custom-call(s32[1]{0:T(128)} %bitcast.me, s32[8]{0:T(128)S(1)} %copy-done.3, s32[1,2]{1,0:T(1,128)S(1)} %collective-permute-done.listed, bf16[768,768]{1,0:T(8,128)(2,1)S(1)} %slice.11.q, bf16[768,768]{1,0:T(8,128)(2,1)S(1)} %slice.9.ko, bf16[768,768]{1,0:T(8,128)(2,1)S(1)} %slice.10.vo, ...), custom_call_target="tpu_custom_call" | custom-call | flops 805306368 | bytes 2359296 | tf_op jit(solution)/shard_map/pallas_call | solution.py:202
  14.9 0.0 copy-start
  14.9 1.7 %collective-permute-start.5 = (bf16[256,256]{1,0:T(8,128)(2,1)S(1)}, bf16[256,256]{1,0:T(8,128)(2,1)S(1)}, u32[]{:S(2)}, u32[]{:S(2)}) collective-permute-start(bf16[256,256]{1,0:T(8,128)(2,1)S(1)} %shard_map.69), channel_id=1, source_target_pairs={{0,8},{1,9},{2,10},{3,11},{4,12},{5,13},{6,14},{7,15},{8,0},{9,1},... | collective-permute-start | bytes 393224 | tf_op jit(solution)/shard_map/ppermute | solution.py:254
  16.6 3.5 %shard_map.70 = bf16[256,512]{1,0:T(8,128)(2,1)S(1)} custom-call(s32[1]{0:T(128)} %bitcast.me, s32[8]{0:T(128)S(1)} %copy-done.3, s32[1,2]{1,0:T(1,128)S(1)} %collective-permute-done.listed, bf16[768,768]{1,0:T(8,128)(2,1)S(1)} %slice.11.q, bf16[768,768]{1,0:T(8,128)(2,1)S(1)} %slice.9.ko, bf16[768,768]{1,0:T(8,128)(2,1)S(1)} %slice.10.vo, ...), custom_call_target="tpu_custom_call" | custom-call | flops 1610612736 | bytes 4718592 | tf_op jit(solution)/shard_map/pallas_call | solution.py:202
  20.1 0.1 collective-permute-start.6
  20.1 0.0 collective-permute-done.3.kx
  20.1 3.2 %collective-permute-done.4.vx = bf16[768,2560]{1,0:T(8,128)(2,1)} collective-permute-done((bf16[768,2560]{1,0:T(8,128)(2,1)}, bf16[768,2560]{1,0:T(8,128)(2,1)}, u32[]{:S(2)}, u32[]{:S(2)}) %collective-permute-start.4) | collective-permute-done | bytes 3932192 | tf_op jit(solution)/shard_map/ppermute | solution.py:244
  23.3 0.0 copy-done
  23.3 5.9 %shard_map.71 = bf16[256,768]{1,0:T(8,128)(2,1)S(1)} custom-call(s32[1]{0:T(128)} %bitcast.me, s32[8]{0:T(128)S(1)} %copy-done.3, s32[1,2]{1,0:T(1,128)S(1)} %collective-permute-done.listed, bf16[768,2560]{1,0:T(8,128)(2,1)S(1)} %copy-done, bf16[768,2560]{1,0:T(8,128)(2,1)} %ko.5, bf16[768,2560]{1,0:T(8,128)(2,1)} %vo.5, ...), custom_call_target="tpu_custom_call" | custom-call | flops 2415919104 | bytes 7077888 | tf_op jit(solution)/shard_map/pallas_call | solution.py:202
  29.3 0.8 %collective-permute-start.7 = (bf16[256,768]{1,0:T(8,128)(2,1)S(1)}, bf16[256,768]{1,0:T(8,128)(2,1)S(1)}, u32[]{:S(2)}, u32[]{:S(2)}) collective-permute-start(bf16[256,768]{1,0:T(8,128)(2,1)S(1)} %shard_map.71), channel_id=1, source_target_pairs={{0,8},{1,9},{2,10},{3,11},{4,12},{5,13},{6,14},{7,15},{8,0},{9,1},... | collective-permute-start | bytes 1179656 | tf_op jit(solution)/shard_map/ppermute | solution.py:254
  30.1 7.2 %shard_map.72 = bf16[256,1024]{1,0:T(8,128)(2,1)S(1)} custom-call(s32[1]{0:T(128)} %bitcast.me, s32[8]{0:T(128)S(1)} %copy-done.3, s32[1,2]{1,0:T(1,128)S(1)} %collective-permute-done.listed, bf16[768,2560]{1,0:T(8,128)(2,1)S(1)} %copy-done, bf16[768,2560]{1,0:T(8,128)(2,1)} %ko.5, bf16[768,2560]{1,0:T(8,128)(2,1)} %vo.5, ...), custom_call_target="tpu_custom_call" | custom-call | flops 3221225472 | bytes 9437184 | tf_op jit(solution)/shard_map/pallas_call | solution.py:202
  37.2 0.1 collective-permute-start.8
  37.3 27.6 %shard_map.68 = bf16[768,2560]{1,0:T(8,128)(2,1)} custom-call(s32[1]{0:T(128)} %bitcast.me, s32[8]{0:T(128)S(1)} %copy-done.3, s32[1,2]{1,0:T(1,128)S(1)} %collective-permute-done.listed, bf16[768,2560]{1,0:T(8,128)(2,1)S(1)} %copy-done, bf16[768,2560]{1,0:T(8,128)(2,1)} %ko.5, bf16[768,2560]{1,0:T(8,128)(2,1)} %vo.5, ...), custom_call_target="tpu_custom_call" | custom-call | flops 16106127360 | bytes 23592960 | tf_op jit(solution)/shard_map/pallas_call | solution.py:202
  64.9 0.0 collective-permute-done.5
  64.9 0.0 collective-permute-done.6
  64.9 0.0 collective-permute-done.7
  64.9 9.7 %collective-permute-done.8 = bf16[256,1024]{1,0:T(8,128)(2,1)S(1)} collective-permute-done((bf16[256,1024]{1,0:T(8,128)(2,1)S(1)}, bf16[256,1024]{1,0:T(8,128)(2,1)S(1)}, u32[]{:S(2)}, u32[]{:S(2)}) %collective-permute-start.8) | collective-permute-done | bytes 524320 | tf_op jit(solution)/shard_map/ppermute | solution.py:254
  74.6 1.1 %pad_maximum_fusion = bf16[256,2560]{1,0:T(8,128)(2,1)} fusion(bf16[256,1024]{1,0:T(8,128)(2,1)S(1)} %collective-permute-done.8, bf16[256,768]{1,0:T(8,128)(2,1)S(1)} %collective-permute-done.7, bf16[256,512]{1,0:T(8,128)(2,1)S(1)} %collective-permute-done.6, bf16[256,256]{1,0:T(8,128)(2,1)S(1)} %collective-permute-done.5), kind=kLoop, calls=%fused_computation | loop fusion | flops 5242880 | bytes 2621440 | tf_op jit(solution)/shard_map/concatenate | solution.py:258
Async XLA Ops:
  0.6 3.4 %copy-start.4 = (s32[1,2]{1,0:T(1,128)S(1)}, s32[1,2]{1,0:T(1,128)}, u32[]{:S(2)}) copy-start(s32[1,2]{1,0:T(1,128)} %param.9) | copy-start | bytes 28
  2.0 10.5 %copy-start.3 = (s32[8]{0:T(128)S(1)}, s32[8]{0:T(128)}, u32[]{:S(2)}) copy-start(s32[8]{0:T(128)} %lengths.9) | copy-start | bytes 100
  2.0 7.6 %collective-permute-start.2 = (bf16[768,768]{1,0:T(8,128)(2,1)S(1)}, bf16[768,768]{1,0:T(8,128)(2,1)S(1)}, u32[]{:S(2)}, u32[]{:S(2)}) collective-permute-start(bf16[768,768]{1,0:T(8,128)(2,1)S(1)} %slice.10.vo), channel_id=1, source_target_pairs={{0,1},{1,0},{2,3},{3,2},{4,5},{5,4},{6,7},{7,6},{8,9},{9,8},{10,11... | collective-permute-start | bytes 3538952 | tf_op jit(solution)/shard_map/ppermute | solution.py:239
  3.9 5.7 %collective-permute-start.1 = (bf16[768,768]{1,0:T(8,128)(2,1)S(1)}, bf16[768,768]{1,0:T(8,128)(2,1)S(1)}, u32[]{:S(2)}, u32[]{:S(2)}) collective-permute-start(bf16[768,768]{1,0:T(8,128)(2,1)S(1)} %slice.9.ko), channel_id=1, source_target_pairs={{0,1},{1,0},{2,3},{3,2},{4,5},{5,4},{6,7},{7,6},{8,9},{9,8},{10,11... | collective-permute-start | bytes 3538952 | tf_op jit(solution)/shard_map/ppermute | solution.py:239
  4.0 5.6 %collective-permute-start = (s32[1,2]{1,0:T(1,128)S(1)}, s32[1,2]{1,0:T(1,128)S(1)}, u32[]{:S(2)}, u32[]{:S(2)}) collective-permute-start(s32[1,2]{1,0:T(1,128)S(1)} %copy-done.4), channel_id=1, source_target_pairs={{0,8},{1,9},{2,10},{3,11},{4,12},{5,13},{6,14},{7,15},{8,0},{9,1},... | collective-permute-start | bytes 32 | tf_op jit(solution)/shard_map/ppermute | solution.py:240
  9.6 1.0 %copy-start.1 = (bf16[768,768]{1,0:T(8,128)(2,1)}, bf16[768,768]{1,0:T(8,128)(2,1)S(1)}, u32[]{:S(2)}) copy-start(bf16[768,768]{1,0:T(8,128)(2,1)S(1)} %collective-permute-done.1.kx) | copy-start | bytes 3538948
  10.6 9.6 %collective-permute-start.3 = (bf16[768,2560]{1,0:T(8,128)(2,1)}, bf16[768,2560]{1,0:T(8,128)(2,1)}, u32[]{:S(2)}, u32[]{:S(2)}) collective-permute-start(bf16[768,2560]{1,0:T(8,128)(2,1)} %ko.5), channel_id=1, source_target_pairs={{0,1},{1,0},{2,3},{3,2},{4,5},{5,4},{6,7},{7,6},{8,9},{9,8},{10,11... | collective-permute-start | bytes 11796488 | tf_op jit(solution)/shard_map/ppermute | solution.py:244
  10.6 12.7 %collective-permute-start.4 = (bf16[768,2560]{1,0:T(8,128)(2,1)}, bf16[768,2560]{1,0:T(8,128)(2,1)}, u32[]{:S(2)}, u32[]{:S(2)}) collective-permute-start(bf16[768,2560]{1,0:T(8,128)(2,1)} %vo.5), channel_id=1, source_target_pairs={{0,1},{1,0},{2,3},{3,2},{4,5},{5,4},{6,7},{7,6},{8,9},{9,8},{10,11... | collective-permute-start | bytes 11796488 | tf_op jit(solution)/shard_map/ppermute | solution.py:244
  11.1 1.6 %copy-start.2 = (bf16[768,768]{1,0:T(8,128)(2,1)S(1)}, bf16[768,768]{1,0:T(8,128)(2,1)}, u32[]{:S(2)}) copy-start(bf16[768,768]{1,0:T(8,128)(2,1)} %copy-done.1) | copy-start | bytes 3538948
  14.9 8.5 %copy-start = (bf16[768,2560]{1,0:T(8,128)(2,1)S(1)}, bf16[768,2560]{1,0:T(8,128)(2,1)}, u32[]{:S(2)}) copy-start(bf16[768,2560]{1,0:T(8,128)(2,1)} %q.5) | copy-start | bytes 11796484
  14.9 50.0 %collective-permute-start.5 = (bf16[256,256]{1,0:T(8,128)(2,1)S(1)}, bf16[256,256]{1,0:T(8,128)(2,1)S(1)}, u32[]{:S(2)}, u32[]{:S(2)}) collective-permute-start(bf16[256,256]{1,0:T(8,128)(2,1)S(1)} %shard_map.69), channel_id=1, source_target_pairs={{0,8},{1,9},{2,10},{3,11},{4,12},{5,13},{6,14},{7,15},{8,0},{9,1},... | collective-permute-start | bytes 393224 | tf_op jit(solution)/shard_map/ppermute | solution.py:254
  20.1 44.9 %collective-permute-start.6 = (bf16[256,512]{1,0:T(8,128)(2,1)S(1)}, bf16[256,512]{1,0:T(8,128)(2,1)S(1)}, u32[]{:S(2)}, u32[]{:S(2)}) collective-permute-start(bf16[256,512]{1,0:T(8,128)(2,1)S(1)} %shard_map.70), channel_id=1, source_target_pairs={{0,8},{1,9},{2,10},{3,11},{4,12},{5,13},{6,14},{7,15},{8,0},{9,1},... | collective-permute-start | bytes 786440 | tf_op jit(solution)/shard_map/ppermute | solution.py:254
  29.3 35.7 %collective-permute-start.7 = (bf16[256,768]{1,0:T(8,128)(2,1)S(1)}, bf16[256,768]{1,0:T(8,128)(2,1)S(1)}, u32[]{:S(2)}, u32[]{:S(2)}) collective-permute-start(bf16[256,768]{1,0:T(8,128)(2,1)S(1)} %shard_map.71), channel_id=1, source_target_pairs={{0,8},{1,9},{2,10},{3,11},{4,12},{5,13},{6,14},{7,15},{8,0},{9,1},... | collective-permute-start | bytes 1179656 | tf_op jit(solution)/shard_map/ppermute | solution.py:254
  37.2 37.4 %collective-permute-start.8 = (bf16[256,1024]{1,0:T(8,128)(2,1)S(1)}, bf16[256,1024]{1,0:T(8,128)(2,1)S(1)}, u32[]{:S(2)}, u32[]{:S(2)}) collective-permute-start(bf16[256,1024]{1,0:T(8,128)(2,1)S(1)} %shard_map.72), channel_id=1, source_target_pairs={{0,8},{1,9},{2,10},{3,11},{4,12},{5,13},{6,14},{7,15},{8,0},{9,1},... | collective-permute-start | bytes 1572872 | tf_op jit(solution)/shard_map/ppermute | solution.py:254

commit v5 on v3

--- a/solution.py
+++ b/solution.py
@@ -16,7 +16,7 @@
 WIDTH = STEP_HEADS * HD
 SCALE = math.log2(math.e) / math.sqrt(HD)
 EARLY_HEADS = (2, 4)
-LATER_HEADS = (6, 8)
+LATER_HEADS = (8, 6)
 HELP_VMEM = 16 << 20
 HOME_VMEM = 26 << 20
 

time: 76.4 us -> 76.5 us (level)
  Pallas kernels: 46.3 us -> 33.3 us
  starting transfers between devices: 7.81 us -> 19.6 us
  waiting for transfers between devices: 14.4 us -> 16 us
    pallas_call x5, Pallas kernels: 46.3 us -> 33.3 us  [call(): pl.pallas_call(body, out_shape=jax.ShapeDtypeStruct((rows, heads * HD), j...]
    ppermute x4, starting transfers between devices: 2.62 us -> 14.4 us  [local(): helped.append(lax.ppermute(outputs, 'seq', far_pairs))]
    ppermute x4, waiting for transfers between devices: 9.7 us -> 12.6 us  [local(): helped.append(lax.ppermute(outputs, 'seq', far_pairs))]
    ppermute x2, waiting for transfers between devices: 3.18 us -> 1.89 us  [local(): kx, vx = lax.ppermute((keys_whole, values_whole), 'seq', core_pairs)]
  transfers between devices with their start and end apart: 9 -> 9, of which waited for: 3 -> 4; matrix products, arithmetic and copies ran while one was open for 4% -> 4% of each run, Pallas kernels for 61% -> 44%
where the time goes in v5:
time: 76.5 us; the launch traced here: 76 us
  Pallas kernels  33.3 us (44%)
  starting transfers between devices  19.6 us (26%)
  waiting for transfers between devices  16 us (21%)
  local copies, waits for them, and re-layouts  5.35 us (7%)
  other arithmetic  1.14 us (1%)
    pallas_call x5, Pallas kernels, call(): pl.pallas_call(body, out_shape=jax.ShapeDtypeStruct((rows, heads * HD), j...  33.3 us
    ppermute x4, starting transfers between devices, local(): helped.append(lax.ppermute(outputs, 'seq', far_pairs))  14.4 us
    ppermute x4, waiting for transfers between devices, local(): helped.append(lax.ppermute(outputs, 'seq', far_pairs))  12.6 us
    slice x3, local copies, waits for them, and re-layouts, local(): q_early, k_early, v_early = (x[:, :early] for x in (queries, keys, values))  4.14 us
    ppermute x1, starting transfers between devices, local(): listed = lax.ppermute(help_table, 'seq', far_pairs)  4.04 us
    ppermute x2, waiting for transfers between devices, local(): kx, vx = lax.ppermute((keys_whole, values_whole), 'seq', core_pairs)  1.89 us
  transfers between devices with their start and end apart: 9, of which 4 were waited for; matrix products, arithmetic and copies ran while one was open for 4% of the time, Pallas kernels for 44%

profile of v5, /device:TPU:0, one launch (start us, length us, event | category | flops | bytes accessed | tf_op | source)
XLA Modules:
  0.0 76.0 jit_solution(10893857786379015802)
XLA Ops:
  0.6 0.0 copy-start.4
  0.6 1.4 %slice.10.vo = bf16[768,768]{1,0:T(8,128)(2,1)S(1)} slice(bf16[768,2560]{1,0:T(8,128)(2,1)} %vo.5), slice={[0:768], [0:768]} | slice | bytes 2359296 | tf_op jit(solution)/shard_map/slice | solution.py:238
  2.0 0.0 copy-start.3
  2.0 0.5 collective-permute-start.2
  2.5 1.3 %slice.9.ko = bf16[768,768]{1,0:T(8,128)(2,1)S(1)} slice(bf16[768,2560]{1,0:T(8,128)(2,1)} %ko.5), slice={[0:768], [0:768]} | slice | bytes 2359296 | tf_op jit(solution)/shard_map/slice | solution.py:238
  3.9 0.1 collective-permute-start.1
  4.0 0.0 copy-done.4
  4.0 4.0 %collective-permute-start = (s32[1,2]{1,0:T(1,128)S(1)}, s32[1,2]{1,0:T(1,128)S(1)}, u32[]{:S(2)}, u32[]{:S(2)}) collective-permute-start(s32[1,2]{1,0:T(1,128)S(1)} %copy-done.4), channel_id=1, source_target_pairs={{0,8},{1,9},{2,10},{3,11},{4,12},{5,13},{6,14},{7,15},{8,0},{9,1},... | collective-permute-start | bytes 32 | tf_op jit(solution)/shard_map/ppermute | solution.py:240
  8.0 1.5 %collective-permute-done.listed = s32[1,2]{1,0:T(1,128)S(1)} collective-permute-done((s32[1,2]{1,0:T(1,128)S(1)}, s32[1,2]{1,0:T(1,128)S(1)}, u32[]{:S(2)}, u32[]{:S(2)}) %collective-permute-start) | collective-permute-done | bytes 40 | tf_op jit(solution)/shard_map/ppermute | solution.py:240
  9.6 0.0 collective-permute-done.2.vx
  9.6 0.0 collective-permute-done.1.kx
  9.6 0.0 copy-start.1
  9.6 1.0 %copy-done.1 = bf16[768,768]{1,0:T(8,128)(2,1)} copy-done((bf16[768,768]{1,0:T(8,128)(2,1)}, bf16[768,768]{1,0:T(8,128)(2,1)S(1)}, u32[]{:S(2)}) %copy-start.1) | copy-done | bytes 1179672
  10.6 0.0 collective-permute-start.3
  10.6 0.5 collective-permute-start.4
  11.1 0.0 copy-start.2
  11.1 1.4 %slice.11.q = bf16[768,768]{1,0:T(8,128)(2,1)S(1)} slice(bf16[768,2560]{1,0:T(8,128)(2,1)} %q.5), slice={[0:768], [0:768]} | slice | bytes 2359296 | tf_op jit(solution)/shard_map/slice | solution.py:238
  12.5 0.0 copy-done.3
  12.5 0.2 copy-done.2
  12.7 0.9 %shard_map.69 = bf16[256,256]{1,0:T(8,128)(2,1)S(1)} custom-call(s32[1]{0:T(128)} %bitcast.me, s32[8]{0:T(128)S(1)} %copy-done.3, s32[1,2]{1,0:T(1,128)S(1)} %collective-permute-done.listed, bf16[768,768]{1,0:T(8,128)(2,1)S(1)} %slice.11.q, bf16[768,768]{1,0:T(8,128)(2,1)S(1)} %slice.9.ko, bf16[768,768]{1,0:T(8,128)(2,1)S(1)} %slice.10.vo, ...), custom_call_target="tpu_custom_call" | custom-call | flops 805306368 | bytes 2359296 | tf_op jit(solution)/shard_map/pallas_call | solution.py:202
  13.6 0.0 copy-start
  13.6 4.3 %collective-permute-start.5 = (bf16[256,256]{1,0:T(8,128)(2,1)S(1)}, bf16[256,256]{1,0:T(8,128)(2,1)S(1)}, u32[]{:S(2)}, u32[]{:S(2)}) collective-permute-start(bf16[256,256]{1,0:T(8,128)(2,1)S(1)} %shard_map.69), channel_id=1, source_target_pairs={{0,8},{1,9},{2,10},{3,11},{4,12},{5,13},{6,14},{7,15},{8,0},{9,1},... | collective-permute-start | bytes 393224 | tf_op jit(solution)/shard_map/ppermute | solution.py:254
  17.9 1.1 %shard_map.70 = bf16[256,512]{1,0:T(8,128)(2,1)S(1)} custom-call(s32[1]{0:T(128)} %bitcast.me, s32[8]{0:T(128)S(1)} %copy-done.3, s32[1,2]{1,0:T(1,128)S(1)} %collective-permute-done.listed, bf16[768,768]{1,0:T(8,128)(2,1)S(1)} %slice.11.q, bf16[768,768]{1,0:T(8,128)(2,1)S(1)} %slice.9.ko, bf16[768,768]{1,0:T(8,128)(2,1)S(1)} %slice.10.vo, ...), custom_call_target="tpu_custom_call" | custom-call | flops 1610612736 | bytes 4718592 | tf_op jit(solution)/shard_map/pallas_call | solution.py:202
  19.0 2.4 %collective-permute-start.6 = (bf16[256,512]{1,0:T(8,128)(2,1)S(1)}, bf16[256,512]{1,0:T(8,128)(2,1)S(1)}, u32[]{:S(2)}, u32[]{:S(2)}) collective-permute-start(bf16[256,512]{1,0:T(8,128)(2,1)S(1)} %shard_map.70), channel_id=1, source_target_pairs={{0,8},{1,9},{2,10},{3,11},{4,12},{5,13},{6,14},{7,15},{8,0},{9,1},... | collective-permute-start | bytes 786440 | tf_op jit(solution)/shard_map/ppermute | solution.py:254
  21.4 0.0 collective-permute-done.3.kx
  21.4 1.9 %collective-permute-done.4.vx = bf16[768,2560]{1,0:T(8,128)(2,1)} collective-permute-done((bf16[768,2560]{1,0:T(8,128)(2,1)}, bf16[768,2560]{1,0:T(8,128)(2,1)}, u32[]{:S(2)}, u32[]{:S(2)}) %collective-permute-start.4) | collective-permute-done | bytes 3932192 | tf_op jit(solution)/shard_map/ppermute | solution.py:244
  23.3 0.0 copy-done
  23.3 3.7 %shard_map.72 = bf16[256,768]{1,0:T(8,128)(2,1)S(1)} custom-call(s32[1]{0:T(128)} %bitcast.me, s32[8]{0:T(128)S(1)} %copy-done.3, s32[1,2]{1,0:T(1,128)S(1)} %collective-permute-done.listed, bf16[768,2560]{1,0:T(8,128)(2,1)S(1)} %copy-done, bf16[768,2560]{1,0:T(8,128)(2,1)} %ko.5, bf16[768,2560]{1,0:T(8,128)(2,1)} %vo.5, ...), custom_call_target="tpu_custom_call" | custom-call | flops 2415919104 | bytes 7077888 | tf_op jit(solution)/shard_map/pallas_call | solution.py:202
  27.1 5.2 %collective-permute-start.8 = (bf16[256,768]{1,0:T(8,128)(2,1)S(1)}, bf16[256,768]{1,0:T(8,128)(2,1)S(1)}, u32[]{:S(2)}, u32[]{:S(2)}) collective-permute-start(bf16[256,768]{1,0:T(8,128)(2,1)S(1)} %shard_map.72), channel_id=1, source_target_pairs={{0,8},{1,9},{2,10},{3,11},{4,12},{5,13},{6,14},{7,15},{8,0},{9,1},... | collective-permute-start | bytes 1179656 | tf_op jit(solution)/shard_map/ppermute | solution.py:254
  32.3 4.8 %shard_map.71 = bf16[256,1024]{1,0:T(8,128)(2,1)S(1)} custom-call(s32[1]{0:T(128)} %bitcast.me, s32[8]{0:T(128)S(1)} %copy-done.3, s32[1,2]{1,0:T(1,128)S(1)} %collective-permute-done.listed, bf16[768,2560]{1,0:T(8,128)(2,1)S(1)} %copy-done, bf16[768,2560]{1,0:T(8,128)(2,1)} %ko.5, bf16[768,2560]{1,0:T(8,128)(2,1)} %vo.5, ...), custom_call_target="tpu_custom_call" | custom-call | flops 3221225472 | bytes 9437184 | tf_op jit(solution)/shard_map/pallas_call | solution.py:202
  37.0 2.5 %collective-permute-start.7 = (bf16[256,1024]{1,0:T(8,128)(2,1)S(1)}, bf16[256,1024]{1,0:T(8,128)(2,1)S(1)}, u32[]{:S(2)}, u32[]{:S(2)}) collective-permute-start(bf16[256,1024]{1,0:T(8,128)(2,1)S(1)} %shard_map.71), channel_id=1, source_target_pairs={{0,8},{1,9},{2,10},{3,11},{4,12},{5,13},{6,14},{7,15},{8,0},{9,1},... | collective-permute-start | bytes 1572872 | tf_op jit(solution)/shard_map/ppermute | solution.py:254
  39.5 22.8 %shard_map.68 = bf16[768,2560]{1,0:T(8,128)(2,1)} custom-call(s32[1]{0:T(128)} %bitcast.me, s32[8]{0:T(128)S(1)} %copy-done.3, s32[1,2]{1,0:T(1,128)S(1)} %collective-permute-done.listed, bf16[768,2560]{1,0:T(8,128)(2,1)S(1)} %copy-done, bf16[768,2560]{1,0:T(8,128)(2,1)} %ko.5, bf16[768,2560]{1,0:T(8,128)(2,1)} %vo.5, ...), custom_call_target="tpu_custom_call" | custom-call | flops 16106127360 | bytes 23592960 | tf_op jit(solution)/shard_map/pallas_call | solution.py:202
  62.3 0.0 collective-permute-done.5
  62.3 0.0 collective-permute-done.6
  62.3 2.0 %collective-permute-done.8 = bf16[256,768]{1,0:T(8,128)(2,1)S(1)} collective-permute-done((bf16[256,768]{1,0:T(8,128)(2,1)S(1)}, bf16[256,768]{1,0:T(8,128)(2,1)S(1)}, u32[]{:S(2)}, u32[]{:S(2)}) %collective-permute-start.8) | collective-permute-done | bytes 393248 | tf_op jit(solution)/shard_map/ppermute | solution.py:254
  64.3 10.6 %collective-permute-done.7 = bf16[256,1024]{1,0:T(8,128)(2,1)S(1)} collective-permute-done((bf16[256,1024]{1,0:T(8,128)(2,1)S(1)}, bf16[256,1024]{1,0:T(8,128)(2,1)S(1)}, u32[]{:S(2)}, u32[]{:S(2)}) %collective-permute-start.7) | collective-permute-done | bytes 524320 | tf_op jit(solution)/shard_map/ppermute | solution.py:254
  74.9 1.1 %pad_maximum_fusion = bf16[256,2560]{1,0:T(8,128)(2,1)} fusion(bf16[256,768]{1,0:T(8,128)(2,1)S(1)} %collective-permute-done.8, bf16[256,1024]{1,0:T(8,128)(2,1)S(1)} %collective-permute-done.7, bf16[256,512]{1,0:T(8,128)(2,1)S(1)} %collective-permute-done.6, bf16[256,256]{1,0:T(8,128)(2,1)S(1)} %collective-permute-done.5), kind=kLoop, calls=%fused_computation | loop fusion | flops 5242880 | bytes 2621440 | tf_op jit(solution)/shard_map/concatenate | solution.py:258
Async XLA Ops:
  0.6 3.4 %copy-start.4 = (s32[1,2]{1,0:T(1,128)S(1)}, s32[1,2]{1,0:T(1,128)}, u32[]{:S(2)}) copy-start(s32[1,2]{1,0:T(1,128)} %param.9) | copy-start | bytes 28
  2.0 10.5 %copy-start.3 = (s32[8]{0:T(128)S(1)}, s32[8]{0:T(128)}, u32[]{:S(2)}) copy-start(s32[8]{0:T(128)} %lengths.9) | copy-start | bytes 100
  2.0 7.6 %collective-permute-start.2 = (bf16[768,768]{1,0:T(8,128)(2,1)S(1)}, bf16[768,768]{1,0:T(8,128)(2,1)S(1)}, u32[]{:S(2)}, u32[]{:S(2)}) collective-permute-start(bf16[768,768]{1,0:T(8,128)(2,1)S(1)} %slice.10.vo), channel_id=1, source_target_pairs={{0,1},{1,0},{2,3},{3,2},{4,5},{5,4},{6,7},{7,6},{8,9},{9,8},{10,11... | collective-permute-start | bytes 3538952 | tf_op jit(solution)/shard_map/ppermute | solution.py:239
  3.9 5.7 %collective-permute-start.1 = (bf16[768,768]{1,0:T(8,128)(2,1)S(1)}, bf16[768,768]{1,0:T(8,128)(2,1)S(1)}, u32[]{:S(2)}, u32[]{:S(2)}) collective-permute-start(bf16[768,768]{1,0:T(8,128)(2,1)S(1)} %slice.9.ko), channel_id=1, source_target_pairs={{0,1},{1,0},{2,3},{3,2},{4,5},{5,4},{6,7},{7,6},{8,9},{9,8},{10,11... | collective-permute-start | bytes 3538952 | tf_op jit(solution)/shard_map/ppermute | solution.py:239
  4.0 5.6 %collective-permute-start = (s32[1,2]{1,0:T(1,128)S(1)}, s32[1,2]{1,0:T(1,128)S(1)}, u32[]{:S(2)}, u32[]{:S(2)}) collective-permute-start(s32[1,2]{1,0:T(1,128)S(1)} %copy-done.4), channel_id=1, source_target_pairs={{0,8},{1,9},{2,10},{3,11},{4,12},{5,13},{6,14},{7,15},{8,0},{9,1},... | collective-permute-start | bytes 32 | tf_op jit(solution)/shard_map/ppermute | solution.py:240
  9.6 1.0 %copy-start.1 = (bf16[768,768]{1,0:T(8,128)(2,1)}, bf16[768,768]{1,0:T(8,128)(2,1)S(1)}, u32[]{:S(2)}) copy-start(bf16[768,768]{1,0:T(8,128)(2,1)S(1)} %collective-permute-done.1.kx) | copy-start | bytes 3538948
  10.6 10.9 %collective-permute-start.3 = (bf16[768,2560]{1,0:T(8,128)(2,1)}, bf16[768,2560]{1,0:T(8,128)(2,1)}, u32[]{:S(2)}, u32[]{:S(2)}) collective-permute-start(bf16[768,2560]{1,0:T(8,128)(2,1)} %ko.5), channel_id=1, source_target_pairs={{0,1},{1,0},{2,3},{3,2},{4,5},{5,4},{6,7},{7,6},{8,9},{9,8},{10,11... | collective-permute-start | bytes 11796488 | tf_op jit(solution)/shard_map/ppermute | solution.py:244
  10.6 12.7 %collective-permute-start.4 = (bf16[768,2560]{1,0:T(8,128)(2,1)}, bf16[768,2560]{1,0:T(8,128)(2,1)}, u32[]{:S(2)}, u32[]{:S(2)}) collective-permute-start(bf16[768,2560]{1,0:T(8,128)(2,1)} %vo.5), channel_id=1, source_target_pairs={{0,1},{1,0},{2,3},{3,2},{4,5},{5,4},{6,7},{7,6},{8,9},{9,8},{10,11... | collective-permute-start | bytes 11796488 | tf_op jit(solution)/shard_map/ppermute | solution.py:244
  11.1 1.6 %copy-start.2 = (bf16[768,768]{1,0:T(8,128)(2,1)S(1)}, bf16[768,768]{1,0:T(8,128)(2,1)}, u32[]{:S(2)}) copy-start(bf16[768,768]{1,0:T(8,128)(2,1)} %copy-done.1) | copy-start | bytes 3538948
  13.6 9.7 %copy-start = (bf16[768,2560]{1,0:T(8,128)(2,1)S(1)}, bf16[768,2560]{1,0:T(8,128)(2,1)}, u32[]{:S(2)}) copy-start(bf16[768,2560]{1,0:T(8,128)(2,1)} %q.5) | copy-start | bytes 11796484
  13.6 48.7 %collective-permute-start.5 = (bf16[256,256]{1,0:T(8,128)(2,1)S(1)}, bf16[256,256]{1,0:T(8,128)(2,1)S(1)}, u32[]{:S(2)}, u32[]{:S(2)}) collective-permute-start(bf16[256,256]{1,0:T(8,128)(2,1)S(1)} %shard_map.69), channel_id=1, source_target_pairs={{0,8},{1,9},{2,10},{3,11},{4,12},{5,13},{6,14},{7,15},{8,0},{9,1},... | collective-permute-start | bytes 393224 | tf_op jit(solution)/shard_map/ppermute | solution.py:254
  19.0 43.3 %collective-permute-start.6 = (bf16[256,512]{1,0:T(8,128)(2,1)S(1)}, bf16[256,512]{1,0:T(8,128)(2,1)S(1)}, u32[]{:S(2)}, u32[]{:S(2)}) collective-permute-start(bf16[256,512]{1,0:T(8,128)(2,1)S(1)} %shard_map.70), channel_id=1, source_target_pairs={{0,8},{1,9},{2,10},{3,11},{4,12},{5,13},{6,14},{7,15},{8,0},{9,1},... | collective-permute-start | bytes 786440 | tf_op jit(solution)/shard_map/ppermute | solution.py:254
  27.1 37.2 %collective-permute-start.8 = (bf16[256,768]{1,0:T(8,128)(2,1)S(1)}, bf16[256,768]{1,0:T(8,128)(2,1)S(1)}, u32[]{:S(2)}, u32[]{:S(2)}) collective-permute-start(bf16[256,768]{1,0:T(8,128)(2,1)S(1)} %shard_map.72), channel_id=1, source_target_pairs={{0,8},{1,9},{2,10},{3,11},{4,12},{5,13},{6,14},{7,15},{8,0},{9,1},... | collective-permute-start | bytes 1179656 | tf_op jit(solution)/shard_map/ppermute | solution.py:254
  37.0 37.9 %collective-permute-start.7 = (bf16[256,1024]{1,0:T(8,128)(2,1)S(1)}, bf16[256,1024]{1,0:T(8,128)(2,1)S(1)}, u32[]{:S(2)}, u32[]{:S(2)}) collective-permute-start(bf16[256,1024]{1,0:T(8,128)(2,1)S(1)} %shard_map.71), channel_id=1, source_target_pairs={{0,8},{1,9},{2,10},{3,11},{4,12},{5,13},{6,14},{7,15},{8,0},{9,1},... | collective-permute-start | bytes 1572872 | tf_op jit(solution)/shard_map/ppermute | solution.py:254
